TPU v7x, 128 devices: a whole 4x4x4 slice. The times are simulated.
128 devices in a mesh: gx: 4 (over y), gy: 32 (over x, z, core).
Axes of the slice: x: 4, y: 4, z: 4, core: 2. Of those that a mesh axis runs over, the one named last changes fastest.
Arguments:
- positions: float32 [3, 2097152], P(None, ('gx', 'gy'))
- panel_weight: float32 [2097152], P(('gx', 'gy')), may hold values from 0.1 to 1
- charges: float32 [8, 2097152], P(None, ('gx', 'gy')), may hold values from -6 to 6
- basis: float32 [16, 2097152], P(None, ('gx', 'gy')), may hold values from -3 to 3
- proxies: float32 [3, 65536], P(None, ('gx', 'gy'))
- local_pairs: int32 [2, 4096], P(None, ('gx', 'gy')), may hold values from 0 to 31, as said below
- cross_pairs: int32 [2, 2048], P(None, ('gx', 'gy')), may hold values from 0 to 31, as said below
- cross_count: int32 [128], P(('gx', 'gy')), may hold values from 0 to 16, as said below
- far_blocks: int32 [2, 32768], P(None, ('gx', 'gy')), may hold values from 0 to 4095, as said below
Outputs:
- potential: float32 [8, 2097152], P(None, ('gx', 'gy'))
Inputs may be any that keep to these rules, and one draw needn't show every extreme that they name: `local_pairs`: both rows hold local cluster indices and the first is smaller than the second. `cross_pairs`: the first row lies in 24 to 31 and the second in 0 to 7; slot 0 of every device pairs its cluster 32 - 1 with the next device's cluster 0. `cross_count`: at least 1 on every device but the last, which has 0; some device has 16. `far_blocks`: the first row holds local clusters, the second global clusters. A device's blocks are listed by owner: its blocks t * 2 to (t + 1) * 2 - 1 have row clusters owned by device t.
All inputs are finite; a program needn't handle non-finite values.
Results may differ from a plain program's by a relative error of at most 0.0003.
Values sent between devices are 32-bit elements; how exact they have to be, the bound alone decides.
A program may use at most 64 MiB of HBM per device.

v0:
```python
import jax
import jax.numpy as jnp
from jax import lax
from jax.sharding import PartitionSpec as P

CLUSTER = 512
RANK = 16
RHS = 8
EDGE = 8


FOUR_PI_INV = 0.07957747154594767
SOFTENING = 0.0025
tile_group = 8


def passed_along(value, axis, steps):
    count = lax.axis_size(axis)
    first, last = (max(0, -steps), min(count, count - steps))
    return lax.ppermute(value, axis, [(source, source + steps) for source in range(first, last)])


def tile_sums(pos_left, charge_left, pos_right, charge_right, first, second, alive, sides):
    highest = lax.Precision.HIGHEST
    total = first.shape[0]
    padding = -total % tile_group
    first = jnp.concatenate([first, jnp.zeros((padding,), jnp.int32)]).reshape(-1, tile_group)
    second = jnp.concatenate([second, jnp.zeros((padding,), jnp.int32)]).reshape(-1, tile_group)
    alive = jnp.concatenate([alive, jnp.zeros((padding,), jnp.float32)]).reshape(-1, tile_group)
    width = pos_left.shape[2]

    def apply_group(sums, item):
        sum_left, sum_right = sums
        idx_first, idx_second, alive_group = item
        pos_first = pos_left[:, idx_first]
        pos_second = pos_right[:, idx_second]
        dist_sq = jnp.sum((pos_first[:, :, :, None] - pos_second[:, :, None, :]) ** 2, axis=0)
        tile = FOUR_PI_INV * lax.rsqrt(dist_sq + SOFTENING) * alive_group[:, None, None]
        sum_left = sum_left.at[:, idx_first].add(
            jnp.einsum("rbq,bpq->rbp", charge_right[:, idx_second], tile, precision=highest)
        )
        if sides != "left":
            sum_right = sum_right.at[:, idx_second].add(
                jnp.einsum("rbp,bpq->rbq", charge_left[:, idx_first], tile, precision=highest)
            )
        return ((sum_left, sum_right), None)

    start = (
        jnp.zeros((RHS, pos_left.shape[1], width), jnp.float32),
        jnp.zeros((RHS, pos_right.shape[1], width), jnp.float32),
    )
    sums, _ = lax.scan(apply_group, start, (first, second, alive))
    return sums


def on_device(
    positions,
    panel_weight,
    charges,
    basis,
    proxies,
    local_pairs,
    cross_pairs,
    cross_count,
    far_blocks,
):
    highest = lax.Precision.HIGHEST
    panels = positions.shape[1]
    own_clusters = panels // CLUSTER
    weighted = charges * panel_weight[None, :]
    pos_blocks = positions.reshape(3, own_clusters, CLUSTER)
    charge_blocks = weighted.reshape(RHS, own_clusters, CLUSTER)
    edge_panels = EDGE * CLUSTER
    head_pos = positions[:, :edge_panels]
    head_charge = weighted[:, :edge_panels]
    next_pos, next_charge = passed_along((head_pos, head_charge), ("gx", "gy"), -1)
    next_pos = next_pos.reshape(3, EDGE, CLUSTER)
    next_charge = next_charge.reshape(RHS, EDGE, CLUSTER)
    self_index = jnp.arange(own_clusters, dtype=jnp.int32)
    self_sum, _ = tile_sums(
        pos_blocks,
        charge_blocks,
        pos_blocks,
        charge_blocks,
        self_index,
        self_index,
        jnp.ones((own_clusters,), jnp.float32),
        "left",
    )
    pair_left, pair_right = tile_sums(
        pos_blocks,
        charge_blocks,
        pos_blocks,
        charge_blocks,
        local_pairs[0],
        local_pairs[1],
        jnp.ones((local_pairs.shape[1],), jnp.float32),
        "both",
    )
    near = self_sum + pair_left + pair_right
    cross_live = (jnp.arange(cross_pairs.shape[1], dtype=jnp.int32) < cross_count[0]).astype(
        jnp.float32
    )
    own_part, next_part = tile_sums(
        pos_blocks,
        charge_blocks,
        next_pos,
        next_charge,
        cross_pairs[0],
        cross_pairs[1],
        cross_live,
        "both",
    )
    returned = passed_along(next_part.reshape(RHS, edge_panels), ("gx", "gy"), 1)
    near = near + own_part
    near = near.at[:, :EDGE].add(returned.reshape(RHS, EDGE, CLUSTER))
    basis_blocks = basis.reshape(RANK, own_clusters, CLUSTER)
    own_coef = jnp.einsum("kcn,rcn->ckr", basis_blocks, charge_blocks, precision=highest)
    table = lax.all_gather(proxies, ("gx", "gy"), axis=1, tiled=True)
    proxy_all = table.reshape(3, -1, RANK)
    proxy_own = proxies.reshape(3, own_clusters, RANK)
    source = far_blocks[0]
    target = far_blocks[1]
    target_proxy = proxy_all[:, target]
    source_proxy = proxy_own[:, source]
    dist_far = jnp.sum((target_proxy[:, :, :, None] - source_proxy[:, :, None, :]) ** 2, axis=0)
    coupling = FOUR_PI_INV * lax.rsqrt(dist_far + SOFTENING)
    contrib = jnp.einsum("bkl,blr->bkr", coupling, own_coef[source], precision=highest).reshape(
        -1, RANK * RHS
    )
    devices = lax.axis_size(("gx", "gy"))
    full_table = (
        jnp.zeros((devices * own_clusters, RANK * RHS), jnp.float32).at[target].add(contrib)
    )
    rowcoef = lax.psum_scatter(full_table, ("gx", "gy"), scatter_dimension=0, tiled=True)
    far = jnp.einsum(
        "kcn,ckr->rcn", basis_blocks, rowcoef.reshape(own_clusters, RANK, RHS), precision=highest
    )
    return panel_weight[None, :] * (near + far).reshape(RHS, panels)


def solution(mesh):
    in_specs = (
        P(None, ("gx", "gy")),
        P(("gx", "gy")),
        P(None, ("gx", "gy")),
        P(None, ("gx", "gy")),
        P(None, ("gx", "gy")),
        P(None, ("gx", "gy")),
        P(None, ("gx", "gy")),
        P(("gx", "gy")),
        P(None, ("gx", "gy")),
    )
    out_specs = P(None, ("gx", "gy"))
    return jax.shard_map(
        on_device, mesh=mesh, in_specs=in_specs, out_specs=out_specs, check_vma=False
    )
```

profile of v0, /device:TPU:0, one launch (start us, length us, event | category | flops | bytes accessed | tf_op | source)
XLA Modules:
  0.0 739.7 jit_solution(8579128332617307284)
XLA Ops:
  11.9 42.5 %all_gather.3 = f32[3,65536]{1,0:T(4,128)S(1)} all-gather(f32[3,512]{1,0:T(4,128)} %param.21), channel_id=1, replica_groups=mesh['gx'=4,'gy'=32] {'gx','gy'}, dimensions={1}, use_global_device_ids=true | all-gather | bytes 792576 | tf_op jit(solution)/shard_map/all_gather | solution.py:119
  61.3 10.8 %copy.55 = f32[3,4096,16]{2,0,1:T(4,128)} copy(f32[3,4096,16]{2,1,0:T(8,128)} %reshape.296) | data formatting | bytes 1572864 | tf_op jit(solution)/shard_map/reshape | solution.py:120
  90.1 111.9 %while.37 = (s32[]{:T(128)}, f32[8,32,512]{2,0,1:T(8,128)S(1)}, f32[8,32,512]{2,0,1:T(8,128)S(1)}, s32[4,8]{1,0:T(4,128)S(1)}, f32[3,32,512]{2,0,1:T(4,128)S(1)}...) while((s32[]{:T(128)}, f32[8,32,512]{2,0,1:T(8,128)S(1)}, f32[8,32,512]{2,0,1:T(8,128)S(1)}, ...), condition=%wide.region_8.9_spmd, body=%wide.region_4.8_spmd.sunk | while | flops 427886656 | bytes 27501024 | solution.py:52
  99.3 9.5 %fusion.75 = f32[8,8,512]{2,1,0:T(8,128)S(1)} fusion(f32[8,512,512]{2,1,0:T(8,128)} %multiply_reduce_fusion.8, f32[8,8,512]{2,1,0:T(8,128)S(1)} %gather_fusion.4), kind=kOutput, calls=%fused_computation.35.clone.1 | convolution fusion | flops 205520896 | bytes 8650752 | tf_op jit(solution)/shard_map/while/body/eval_jaxpr/rbq,bpq->rbp/dot_general | solution.py:40
  110.2 7.2 fusion.76
  127.2 9.5 %fusion.75 = f32[8,8,512]{2,1,0:T(8,128)S(1)} fusion(f32[8,512,512]{2,1,0:T(8,128)} %multiply_reduce_fusion.8, f32[8,8,512]{2,1,0:T(8,128)S(1)} %gather_fusion.4), kind=kOutput, calls=%fused_computation.35.clone.1 | convolution fusion | flops 205520896 | bytes 8650752 | tf_op jit(solution)/shard_map/while/body/eval_jaxpr/rbq,bpq->rbp/dot_general | solution.py:40
  138.1 7.2 fusion.76
  155.1 9.5 %fusion.75 = f32[8,8,512]{2,1,0:T(8,128)S(1)} fusion(f32[8,512,512]{2,1,0:T(8,128)} %multiply_reduce_fusion.8, f32[8,8,512]{2,1,0:T(8,128)S(1)} %gather_fusion.4), kind=kOutput, calls=%fused_computation.35.clone.1 | convolution fusion | flops 205520896 | bytes 8650752 | tf_op jit(solution)/shard_map/while/body/eval_jaxpr/rbq,bpq->rbp/dot_general | solution.py:40
  166.0 7.2 fusion.76
  183.0 9.5 %fusion.75 = f32[8,8,512]{2,1,0:T(8,128)S(1)} fusion(f32[8,512,512]{2,1,0:T(8,128)} %multiply_reduce_fusion.8, f32[8,8,512]{2,1,0:T(8,128)S(1)} %gather_fusion.4), kind=kOutput, calls=%fused_computation.35.clone.1 | convolution fusion | flops 205520896 | bytes 8650752 | tf_op jit(solution)/shard_map/while/body/eval_jaxpr/rbq,bpq->rbp/dot_general | solution.py:40
  194.0 7.2 fusion.76
  202.1 74.7 %while.36 = (s32[]{:T(128)}, f32[8,32,512]{2,0,1:T(8,128)S(1)}, s32[4,8]{1,0:T(4,128)S(1)}, f32[3,32,512]{2,0,1:T(4,128)S(1)}, f32[8,32,512]{2,0,1:T(8,128)S(1)}, /*index=5*/s32[]{:T(128)}) while((s32[]{:T(128)}, f32[8,32,512]{2,0,1:T(8,128)S(1)}, s32[4,8]{1,0:T(4,128)S(1)}, f32[3,32,512]{2,0,1:T(4,128)S(1)}, f32[8,32,512]{2,0,1:T(8,128)S(1)}, ...), condition=%wide.region_3.4_spmd, body=%wide.region_0.3_spmd.sunk | while | flops 222331936 | bytes 17944848 | solution.py:52
  202.7 7.1 multiply_reduce_fusion.7
  210.4 9.5 %fusion.71 = f32[8,8,512]{2,1,0:T(8,128)S(1)} fusion(f32[8,512,512]{2,1,0:T(8,128)} %multiply_reduce_fusion.7, f32[8,8,512]{2,1,0:T(8,128)S(1)} %gather_fusion.1), kind=kOutput, calls=%fused_computation.20.clone.1 | convolution fusion | flops 205520896 | bytes 8650752 | tf_op jit(solution)/shard_map/while/body/eval_jaxpr/rbq,bpq->rbp/dot_general | solution.py:40
  221.4 7.1 multiply_reduce_fusion.7
  229.1 9.5 %fusion.71 = f32[8,8,512]{2,1,0:T(8,128)S(1)} fusion(f32[8,512,512]{2,1,0:T(8,128)} %multiply_reduce_fusion.7, f32[8,8,512]{2,1,0:T(8,128)S(1)} %gather_fusion.1), kind=kOutput, calls=%fused_computation.20.clone.1 | convolution fusion | flops 205520896 | bytes 8650752 | tf_op jit(solution)/shard_map/while/body/eval_jaxpr/rbq,bpq->rbp/dot_general | solution.py:40
  247.8 9.5 %fusion.71 = f32[8,8,512]{2,1,0:T(8,128)S(1)} fusion(f32[8,512,512]{2,1,0:T(8,128)} %multiply_reduce_fusion.7, f32[8,8,512]{2,1,0:T(8,128)S(1)} %gather_fusion.1), kind=kOutput, calls=%fused_computation.20.clone.1 | convolution fusion | flops 205520896 | bytes 8650752 | tf_op jit(solution)/shard_map/while/body/eval_jaxpr/rbq,bpq->rbp/dot_general | solution.py:40
  266.4 9.5 %fusion.71 = f32[8,8,512]{2,1,0:T(8,128)S(1)} fusion(f32[8,512,512]{2,1,0:T(8,128)} %multiply_reduce_fusion.7, f32[8,8,512]{2,1,0:T(8,128)S(1)} %gather_fusion.1), kind=kOutput, calls=%fused_computation.20.clone.1 | convolution fusion | flops 205520896 | bytes 8650752 | tf_op jit(solution)/shard_map/while/body/eval_jaxpr/rbq,bpq->rbp/dot_general | solution.py:40
  279.4 58.8 %while.38 = (s32[]{:T(128)}, f32[8,32,512]{2,0,1:T(8,128)S(1)}, f32[8,8,512]{2,0,1:T(8,128)S(1)}, s32[2,8]{1,0:T(2,128)}, f32[3,32,512]{2,0,1:T(4,128)S(1)}, /*i...) while((s32[]{:T(128)}, f32[8,32,512]{2,0,1:T(8,128)S(1)}, ...), condition=%wide.region_13.14_spmd, body=%wide.region_9.13_spmd.sunk | while | flops 427886656 | bytes 27501180 | solution.py:52
  289.9 9.5 %fusion.81 = f32[8,8,512]{2,1,0:T(8,128)S(1)} fusion(f32[8,512,512]{2,1,0:T(8,128)} %multiply_reduce_fusion.9, f32[8]{0:T(128)S(1)} %fusion.80, f32[8,8,512]{2,1,0:T(8,128)S(1)} %gather_fusion.8), kind=kOutput, calls=%fused_computation.55.clone.1 | convolution fusion | flops 205520896 | bytes 8650784 | tf_op jit(solution)/shard_map/while/body/eval_jaxpr/rbq,bpq->rbp/dot_general | solution.py:40
  300.9 7.2 fusion.82
  319.2 9.5 %fusion.81 = f32[8,8,512]{2,1,0:T(8,128)S(1)} fusion(f32[8,512,512]{2,1,0:T(8,128)} %multiply_reduce_fusion.9, f32[8]{0:T(128)S(1)} %fusion.80, f32[8,8,512]{2,1,0:T(8,128)S(1)} %gather_fusion.8), kind=kOutput, calls=%fused_computation.55.clone.1 | convolution fusion | flops 205520896 | bytes 8650784 | tf_op jit(solution)/shard_map/while/body/eval_jaxpr/rbq,bpq->rbp/dot_general | solution.py:40
  330.1 7.2 fusion.82
  341.5 387.7 %reduce-scatter.2.cloned.1.call-done = f32[32,128]{1,0:T(8,128)} async-done(((f32[4096,128]{1,0:T(8,128)}), f32[32,128]{1,0:T(8,128)}) %reduce-scatter.2.cloned.1.call-update) | async-done | bytes 16400 | tf_op jit(solution)/shard_map/reduce_scatter | solution.py:135
  (159 shorter events, 130.7 us)
Async XLA Ops:
  6.5 722.6 %reduce-scatter.2.cloned.1.call-start = ((), (), s32[]{:S(2)}) async-start(), calls=%async_computation.1 | async-start | bytes 2113536 | tf_op jit(solution)/shard_map/reduce_scatter | solution.py:135
  7.4 271.9 %collective-permute-start = (f32[3,4096]{1,0:T(4,128)S(1)}, f32[3,4096]{1,0:T(4,128)S(1)}, u32[]{:S(2)}, u32[]{:S(2)}) collective-permute-start(f32[3,4096]{1,0:T(4,128)S(1)} %slice.52), channel_id=1, source_target_pairs={{1,0},{2,1},{3,2},{4,3},{5,4},{6,5},{7,6},{8,7},{9,8},{10,9},{11,1... | collective-permute-start | bytes 147464 | tf_op jit(solution)/shard_map/ppermute | solution.py:20
  9.8 269.5 %collective-permute-start.1 = (f32[8,4096]{1,0:T(8,128)S(1)}, f32[8,4096]{1,0:T(8,128)S(1)}, u32[]{:S(2)}, u32[]{:S(2)}) collective-permute-start(f32[8,4096]{1,0:T(8,128)S(1)} %slice.83), channel_id=1, source_target_pairs={{1,0},{2,1},{3,2},{4,3},{5,4},{6,5},{7,6},{8,7},{9,8},{10,9},{11,1... | collective-permute-start | bytes 393224 | tf_op jit(solution)/shard_map/ppermute | solution.py:20
  61.3 17.9 %copy-start.1 = (f32[16,16384]{1,0:T(8,128)S(1)}, f32[16,16384]{1,0:T(8,128)}, u32[]{:S(2)}) copy-start(f32[16,16384]{1,0:T(8,128)} %param.20) | copy-start | bytes 3145732
  79.2 10.6 %copy-start.3 = (s32[2,32]{1,0:T(2,128)S(1)}, s32[2,32]{1,0:T(2,128)}, u32[]{:S(2)}) copy-start(s32[2,32]{1,0:T(2,128)} %param.22) | copy-start | bytes 772
  79.2 10.9 %copy-start = (f32[3,16384]{1,0:T(4,128)S(1)}, f32[3,16384]{1,0:T(4,128)}, u32[]{:S(2)}) copy-start(f32[3,16384]{1,0:T(4,128)} %param.17) | copy-start | bytes 589828
  202.1 74.7 %copy-start.4 = (s32[2,16]{1,0:T(2,128)S(1)}, s32[2,16]{1,0:T(2,128)}, u32[]{:S(2)}) copy-start(s32[2,16]{1,0:T(2,128)} %param.23) | copy-start | bytes 388
  279.3 452.6 %copy-start.2 = (f32[16384]{0:T(1024)S(1)}, f32[16384]{0:T(1024)}, u32[]{:S(2)}) copy-start(f32[16384]{0:T(1024)} %param.18) | copy-start | bytes 196612
  338.2 3.3 collective-permute-start.2
Sparse Core Ops, SparseCore 0:
  89.9 639.2 reduce-scatter.1
where the time goes:
time: 740 us
  waiting for transfers between devices  388 us (52%)
  matrix products  146 us (20%)
  other arithmetic  93.8 us (13%)
  local copies, waits for them, and re-layouts  48.3 us (7%)
  blocking collectives  42.5 us (6%)
  between operations  14.3 us (2%)
    reduce_scatter x1, waiting for transfers between devices, on_device(): lax.psum_scatter(full_table, ('gx', 'gy'), scatter_dimension=0, tiled=True)  388 us
    dot_general x10, matrix products, apply_group(): jnp.einsum('rbq,bpq->rbp', charge_right[:, idx_second], tile, precision=h...  95 us
    reduce_sum x10, other arithmetic, apply_group(): jnp.sum((pos_first[:, :, :, None] - pos_second[:, :, None, :]) ** 2, axis=0)  71.1 us
    dot_general x6, matrix products, apply_group(): jnp.einsum('rbp,bpq->rbq', charge_left[:, idx_first], tile, precision=hig...  43.3 us
    all_gather x1, blocking collectives, on_device(): table = lax.all_gather(proxies, ('gx', 'gy'), axis=1, tiled=True)  42.5 us
    reshape x2, local copies, waits for them, and re-layouts, on_device(): proxy_all = table.reshape(3, -1, RANK)  15.7 us
  transfers between devices with their start and end apart: 4, of which 2 were waited for; matrix products, arithmetic and copies ran while one was open for 38% of the time, Pallas kernels for 0%

commit v1 on v0

v1 whole, which is shorter than its diff:
```python
import functools

import jax
import jax.numpy as jnp
from jax import lax
from jax.experimental import pallas as pl
from jax.experimental.pallas import tpu as pltpu
from jax.sharding import PartitionSpec as P

CLUSTER = 512
RANK = 16
RHS = 8
EDGE = 8
FOUR_PI_INV = 0.07957747154594767
SOFTENING = 0.0025
CL_DEV = 32
LOC_DEV = 32
CROSS_DEV = 16
FAR_DEV = 256
EDGE_PANELS = EDGE * CLUSTER
CHUNK = 32
DEVICES = 128
N_Y, N_X, N_ZC = 4, 4, 8
ROWS = 8
MESH = pl.DeviceIdType.MESH
F32 = jnp.float32
BF16 = jnp.bfloat16


def dot(a, b, dims):
    return lax.dot_general(a, b, ((dims[:1], dims[1:]), ((), ())), preferred_element_type=F32)


def split(value, parts):
    out = []
    for _ in range(parts - 1):
        high = value.astype(BF16)
        out.append(high)
        value = value - high.astype(F32)
    out.append(value.astype(BF16))
    return out


def panels_of(cluster):
    return pl.ds(pl.multiple_of(cluster * CLUSTER, CLUSTER), CLUSTER)


def split_rows(value):
    high = value.astype(BF16).astype(F32)
    return jnp.concatenate([high, value - high], axis=0).astype(BF16)


def near_kernel(
    pos, weight, charges, basis, proxy_table, ids, local_pairs, cross_pairs, cross_mask,
    self_sum, first_sum, second_sum, cross_sum, far_in, returned,
    cw, pos_c, pos_t, moments, send, recv1, recv2, head_w, next_pos, next_w, next_pos_c, next_cw, back, tile_hi, tile_lo,
    far_send, far_recv, far_own, edge_send, edge_recv,
):
    y = lax.axis_index("gx")
    gy = lax.axis_index("gy")
    x = gy // N_ZC
    zc = lax.rem(gy, N_ZC)
    flat = y * (N_X * N_ZC) + gy

    def device_of(index):
        return (index // (N_X * N_ZC), lax.rem(index, N_X * N_ZC))

    after = device_of(lax.rem(flat + 1, DEVICES))
    before = device_of(lax.rem(flat + DEVICES - 1, DEVICES))
    peers = (
        [(lax.rem(y + i, N_Y), gy) for i in range(1, N_Y)]
        + [(y, lax.rem(x + i, N_X) * N_ZC + zc) for i in range(1, N_X)]
        + [(y, x * N_ZC + lax.rem(zc + i, N_ZC)) for i in range(1, N_ZC)]
    )
    barrier = pltpu.get_barrier_semaphore()
    for peer in peers + [after, before]:
        pl.semaphore_signal(barrier, inc=1, device_id=peer, device_id_type=MESH)

    def prepare(c, carry):
        cols = panels_of(c)
        weighted = charges[:, cols] * weight[:, cols]
        parts = split_rows(weighted)
        cw[c] = parts
        place = jnp.concatenate([pos[:, cols], jnp.zeros((5, CLUSTER), F32)], axis=0)
        pos_c[c] = place
        pos_t[c] = place.T
        moments[pl.ds(pl.multiple_of(c * 32, 32), 32), :] = dot(split_rows(basis[:, cols]), parts, (1, 1))
        return carry

    lax.fori_loop(0, CL_DEV, prepare, 0)
    head_w[...] = charges[:, :EDGE_PANELS] * weight[:, :EDGE_PANELS]

    row = lax.broadcasted_iota(jnp.int32, (2 * RHS, 128), 0)
    lane = lax.broadcasted_iota(jnp.int32, (2 * RHS, 128), 1)
    spread = jnp.where(lax.rem(row, RHS) == lax.rem(lane, RHS), 1.0, 0.0).astype(BF16)
    wide = sum(dot(part, spread, (1, 0)) for part in split(moments[...], 3))
    row = lax.broadcasted_iota(jnp.int32, wide.shape, 0)
    lane = lax.broadcasted_iota(jnp.int32, wide.shape, 1)
    wide = jnp.where(lax.rem(row, RANK) == lane // RHS, wide, 0.0)
    coef = jnp.sum(wide.reshape(CL_DEV, 2 * RANK, 128), axis=1)

    coef_parts = split(coef, 3)
    proxy_parts = split(proxy_table[...], 3)
    row = lax.broadcasted_iota(jnp.int32, (32, 128), 0)
    lane = lax.broadcasted_iota(jnp.int32, (32, 128), 1)
    numbers = jnp.where(lane == 3 * RANK, row.astype(F32), 0.0).astype(BF16)
    table = jnp.concatenate(
        [coef_parts[0], proxy_parts[0], coef_parts[1], proxy_parts[1], coef_parts[2], proxy_parts[2], numbers],
        axis=0,
    )
    row = lax.broadcasted_iota(jnp.int32, (192, 1), 0)
    pick_table = jnp.where(lax.rem(row, 64) == ids[0:1, :], 1.0, 0.0)
    row = lax.broadcasted_iota(jnp.int32, (32, 1), 0)
    pick_number = jnp.where(row == ids[1:2, :], 1.0, 0.0)
    pick = jnp.concatenate([pick_table, pick_number], axis=0).astype(BF16)
    send[...] = dot(pick, table, (0, 0)).reshape(send.shape)

    def far_copy(source, target, index, peer):
        return pltpu.make_async_remote_copy(
            src_ref=source, dst_ref=target, send_sem=far_send.at[index], recv_sem=far_recv.at[index],
            device_id=peer, device_id_type=MESH,
        )

    def edge_copy(source, target, index, peer):
        return pltpu.make_async_remote_copy(
            src_ref=source, dst_ref=target, send_sem=edge_send.at[index], recv_sem=edge_recv.at[index],
            device_id=peer, device_id_type=MESH,
        )

    def start(copies):
        for copy in copies:
            copy.start()

    def wait(copies):
        for copy in copies:
            copy.wait()

    phase1 = [pltpu.make_async_copy(send.at[y], recv1.at[0], far_own.at[0])] + [
        far_copy(send.at[lax.rem(y + i, N_Y)], recv1.at[i], i - 1, peers[i - 1]) for i in range(1, N_Y)
    ]
    phase2 = [pltpu.make_async_copy(recv1.at[:, x], recv2.at[0], far_own.at[1])] + [
        far_copy(recv1.at[:, lax.rem(x + i, N_X)], recv2.at[i], 2 + i, peers[2 + i]) for i in range(1, N_X)
    ]
    phase3 = [pltpu.make_async_copy(recv2.at[:, :, zc], far_in.at[0], far_own.at[2])] + [
        far_copy(recv2.at[:, :, lax.rem(zc + i, N_ZC)], far_in.at[i], 5 + i, peers[5 + i]) for i in range(1, N_ZC)
    ]
    heads = [
        edge_copy(pos.at[:, pl.ds(0, EDGE_PANELS)], next_pos, 0, before),
        edge_copy(head_w, next_w, 1, before),
    ]
    give_back = [edge_copy(back, returned, 2, after)]

    pl.semaphore_wait(barrier, len(peers) + 2)
    start(heads)
    start(phase1)

    def tile(row_cluster, columns, slot):
        col_x, col_y, col_z = columns[0:1, :], columns[1:2, :], columns[2:3, :]
        for i in range(CLUSTER // CHUNK):
            rows = pos_t[row_cluster, i * CHUNK : (i + 1) * CHUNK, :]
            dx = rows[:, 0:1] - col_x
            dy = rows[:, 1:2] - col_y
            dz = rows[:, 2:3] - col_z
            value = lax.rsqrt(dx * dx + dy * dy + dz * dz + SOFTENING)
            high = value.astype(BF16)
            tile_hi[slot, i * CHUNK : (i + 1) * CHUNK, :] = high
            tile_lo[slot, i * CHUNK : (i + 1) * CHUNK, :] = (value - high.astype(F32)).astype(BF16)

    def applied(parts, slot, side):
        sums = dot(parts, tile_hi[slot], (1, side)) + dot(parts, tile_lo[slot], (1, side))
        return sums[:RHS] + sums[RHS:]

    def section(count, compute, apply):
        compute(0, 0)

        def body(i, carry):
            compute(2 * i + 1, 1)
            apply(2 * i, 0)
            compute(jnp.minimum(2 * i + 2, count - 1), 0)
            apply(2 * i + 1, 1)
            return carry

        lax.fori_loop(0, count // 2, body, 0)

    def self_compute(t, slot):
        tile(t, pos_c[t], slot)

    def self_apply(t, slot):
        self_sum[:, panels_of(t)] = applied(cw[t], slot, 0)

    section(CL_DEV, self_compute, self_apply)

    wait(phase1)
    start(phase2)
    wait(heads)
    for j in range(EDGE):
        cols = slice(j * CLUSTER, (j + 1) * CLUSTER)
        next_cw[j] = split_rows(next_w[:, cols])
        next_pos_c[j, 0:3, :] = next_pos[:, cols]
    back[...] = jnp.zeros_like(back)

    def cross_compute(t, slot):
        tile(cross_pairs[0, t], next_pos_c[cross_pairs[1, t]], slot)

    def cross_apply(t, slot):
        cross_sum[t] = applied(next_cw[cross_pairs[1, t]], slot, 1) * cross_mask[EDGE, t]
        product = applied(cw[cross_pairs[0, t]], slot, 0)
        for j in range(EDGE):
            back[j] += product * cross_mask[j, t]

    section(CROSS_DEV, cross_compute, cross_apply)
    start(give_back)
    wait(phase2)
    start(phase3)

    def local_compute(t, slot):
        tile(local_pairs[0, t], pos_c[local_pairs[1, t]], slot)

    def local_apply(t, slot):
        first_sum[t] = applied(cw[local_pairs[1, t]], slot, 1)
        second_sum[t] = applied(cw[local_pairs[0, t]], slot, 0)

    section(LOC_DEV, local_compute, local_apply)
    wait(phase3)
    wait(give_back)


def far_kernel(
    far_in, proxy_table, basis, weight, self_sum, first_sum, second_sum, cross_sum, returned,
    local_pairs, cross_pairs, out, rows_ref,
):
    def strided(j):
        return far_in[pl.ds(j, DEVICES, stride=ROWS), :]

    coef = jnp.concatenate([strided(0), strided(1)], axis=0)
    source = jnp.concatenate([strided(2), strided(3)], axis=0)
    lane = lax.broadcasted_iota(jnp.int32, (FAR_DEV, 128), 1)
    number = jnp.sum(jnp.where(lane == 3 * RANK, source, 0.0), axis=1, keepdims=True).astype(jnp.int32)
    lane = lax.broadcasted_iota(jnp.int32, (FAR_DEV, CL_DEV), 1)
    pick = jnp.where(lane == number, 1.0, 0.0).astype(BF16)
    target = sum(dot(pick, part, (1, 0)) for part in split(proxy_table[...], 3))
    row = lax.broadcasted_iota(jnp.int32, (128, 3 * 256), 0)
    lane = lax.broadcasted_iota(jnp.int32, (128, 3 * 256), 1)
    axis = lane // 256
    from_target = jnp.where(row == axis * RANK + lax.rem(lane, 256) // RANK, 1.0, 0.0).astype(BF16)
    from_source = jnp.where(row == axis * RANK + lax.rem(lane, RANK), -1.0, 0.0).astype(BF16)
    offsets = sum(dot(part, from_target, (1, 0)) for part in split(target, 3))
    offsets = offsets + sum(dot(part, from_source, (1, 0)) for part in split(source, 3))
    offsets = offsets * offsets
    coupling = lax.rsqrt(offsets[:, :256] + offsets[:, 256:512] + offsets[:, 512:] + SOFTENING)
    coupling_parts = split(coupling, 2)
    coef_parts = split(coef, 2)
    contrib = jnp.zeros((FAR_DEV, 128), F32)
    for l in range(RANK):
        row = lax.broadcasted_iota(jnp.int32, (256, 128), 0)
        lane = lax.broadcasted_iota(jnp.int32, (256, 128), 1)
        widen = jnp.where(row == (lane // RHS) * RANK + l, 1.0, 0.0).astype(BF16)
        row = lax.broadcasted_iota(jnp.int32, (128, 128), 0)
        lane = lax.broadcasted_iota(jnp.int32, (128, 128), 1)
        repeat = jnp.where(row == l * RHS + lax.rem(lane, RHS), 1.0, 0.0).astype(BF16)
        left = sum(dot(part, widen, (1, 0)) for part in coupling_parts)
        right = sum(dot(part, repeat, (1, 0)) for part in coef_parts)
        contrib = contrib + left * right
    rowcoef = sum(dot(pick, part, (0, 0)) for part in split(contrib, 3))
    row = lax.broadcasted_iota(jnp.int32, (CL_DEV * RHS, CL_DEV), 0)
    lane = lax.broadcasted_iota(jnp.int32, (CL_DEV * RHS, CL_DEV), 1)
    eight = jnp.where(row // RHS == lane, 1.0, 0.0).astype(BF16)
    wide = sum(dot(eight, part, (1, 0)) for part in split(rowcoef, 3))
    row = lax.broadcasted_iota(jnp.int32, wide.shape, 0)
    lane = lax.broadcasted_iota(jnp.int32, wide.shape, 1)
    wide = jnp.where(lax.rem(row, RHS) == lax.rem(lane, RHS), wide, 0.0)
    row = lax.broadcasted_iota(jnp.int32, (128, RANK), 0)
    lane = lax.broadcasted_iota(jnp.int32, (128, RANK), 1)
    narrow = jnp.where(row // RHS == lane, 1.0, 0.0).astype(BF16)
    rows_ref[...] = sum(dot(part, narrow, (1, 0)) for part in split(wide, 3))

    def start(c, carry):
        cols = panels_of(c)
        block = basis[:, cols]
        high = block.astype(BF16).astype(F32)
        blocks = jnp.concatenate([high, block - high, high], axis=0).astype(BF16)
        left = rows_ref[pl.ds(pl.multiple_of(c * RHS, RHS), RHS), :]
        left_high = left.astype(BF16).astype(F32)
        lefts = jnp.concatenate([left_high, left_high, left - left_high], axis=1).astype(BF16)
        out[:, cols] = self_sum[:, cols] + dot(lefts, blocks, (1, 0))
        return carry

    lax.fori_loop(0, CL_DEV, start, 0)
    for j in range(EDGE):
        out[:, j * CLUSTER : (j + 1) * CLUSTER] += returned[j]

    def add_local(t, carry):
        out[:, panels_of(local_pairs[0, t])] += first_sum[t]
        out[:, panels_of(local_pairs[1, t])] += second_sum[t]
        return carry

    lax.fori_loop(0, LOC_DEV, add_local, 0)

    def add_cross(t, carry):
        out[:, panels_of(cross_pairs[0, t])] += cross_sum[t]
        return carry

    lax.fori_loop(0, CROSS_DEV, add_cross, 0)
    out[...] = out[...] * (weight[...] * FOUR_PI_INV)


def on_device(
    positions, panel_weight, charges, basis, proxies, local_pairs, cross_pairs, cross_count, far_blocks
):
    panels = positions.shape[1]
    weight = panel_weight.reshape(1, panels)
    proxy_table = proxies.reshape(3, CL_DEV, RANK).transpose(1, 0, 2).reshape(CL_DEV, 3 * RANK)
    proxy_table = jnp.pad(proxy_table, ((0, 0), (0, 128 - 3 * RANK)))
    source = far_blocks[0].reshape(DEVICES, 2)
    local_row = lax.rem(far_blocks[1], CL_DEV).reshape(DEVICES, 2)
    none = jnp.full((DEVICES, 2), -1, jnp.int32)
    table_ids = jnp.concatenate([source, source + CL_DEV, none, none], axis=1).reshape(1, -1)
    number_ids = jnp.concatenate([none, local_row, none, none], axis=1).reshape(1, -1)
    ids = jnp.concatenate([table_ids, number_ids], axis=0)
    alive = jnp.arange(CROSS_DEV, dtype=jnp.int32)[None, :] < cross_count[0]
    edge = jnp.arange(EDGE + 1, dtype=jnp.int32)[:, None]
    cross_mask = ((edge == cross_pairs[1:2, :]) | (edge == EDGE)) & alive
    cross_mask = cross_mask.astype(F32)

    vmem = pl.BlockSpec(memory_space=pltpu.VMEM)
    smem = pl.BlockSpec(memory_space=pltpu.SMEM)
    block = functools.partial(pltpu.VMEM, dtype=F32)
    outs = pl.pallas_call(
        near_kernel,
        out_shape=[
            jax.ShapeDtypeStruct(shape, F32)
            for shape in (
                (RHS, panels),
                (LOC_DEV, RHS, CLUSTER),
                (LOC_DEV, RHS, CLUSTER),
                (CROSS_DEV, RHS, CLUSTER),
                (N_ZC, N_X, N_Y, ROWS, 128),
                (EDGE, RHS, CLUSTER),
            )
        ],
        in_specs=[vmem] * 6 + [smem] * 3,
        out_specs=[vmem] * 6,
        scratch_shapes=[
            pltpu.VMEM((CL_DEV, 2 * RHS, CLUSTER), BF16),
            pltpu.VMEM((CL_DEV, 8, CLUSTER), F32),
            pltpu.VMEM((CL_DEV, CLUSTER, 8), F32),
            pltpu.VMEM((CL_DEV * 2 * RANK, 2 * RHS), F32),
            pltpu.VMEM((N_Y, N_X, N_ZC, ROWS, 128), F32),
            pltpu.VMEM((N_Y, N_X, N_ZC, ROWS, 128), F32),
            pltpu.VMEM((N_X, N_Y, N_ZC, ROWS, 128), F32),
            pltpu.VMEM((RHS, EDGE_PANELS), F32),
            pltpu.VMEM((3, EDGE_PANELS), F32),
            pltpu.VMEM((RHS, EDGE_PANELS), F32),
            pltpu.VMEM((EDGE, 8, CLUSTER), F32),
            pltpu.VMEM((EDGE, 2 * RHS, CLUSTER), BF16),
            pltpu.VMEM((EDGE, RHS, CLUSTER), F32),
            pltpu.VMEM((2, CLUSTER, CLUSTER), BF16),
            pltpu.VMEM((2, CLUSTER, CLUSTER), BF16),
            pltpu.SemaphoreType.DMA((13,)),
            pltpu.SemaphoreType.DMA((13,)),
            pltpu.SemaphoreType.DMA((3,)),
            pltpu.SemaphoreType.DMA((3,)),
            pltpu.SemaphoreType.DMA((3,)),
        ],
        compiler_params=pltpu.CompilerParams(
            collective_id=0, has_side_effects=True, vmem_limit_bytes=48 * 2**20
        ),
    )(positions, weight, charges, basis, proxy_table, ids, local_pairs, cross_pairs, cross_mask)
    self_sum, first_sum, second_sum, cross_sum, far_in, returned = outs
    return pl.pallas_call(
        far_kernel,
        out_shape=jax.ShapeDtypeStruct((RHS, panels), F32),
        in_specs=[vmem] * 9 + [smem] * 2,
        out_specs=vmem,
        scratch_shapes=[pltpu.VMEM((CL_DEV * RHS, RANK), F32)],
        compiler_params=pltpu.CompilerParams(vmem_limit_bytes=48 * 2**20),
    )(
        far_in.reshape(-1, 128), proxy_table, basis, weight, self_sum, first_sum, second_sum, cross_sum,
        returned, local_pairs, cross_pairs,
    )


def solution(mesh):
    whole = P(None, ("gx", "gy"))
    flat = P(("gx", "gy"))
    return jax.shard_map(
        on_device,
        mesh=mesh,
        in_specs=(whole, flat, whole, whole, whole, whole, whole, flat, whole),
        out_specs=whole,
        check_vma=False,
    )
```

time: 740 us -> 74.7 us (0.10)
  waiting for transfers between devices: 388 us -> 0 us
  matrix products: 146 us -> 0 us
  other arithmetic: 93.8 us -> 0.22 us
  Pallas kernels: 0 us -> 67.7 us
  local copies, waits for them, and re-layouts: 48.3 us -> 5.61 us
  blocking collectives: 42.5 us -> 0 us
  between operations: 14.3 us -> 0.84 us
    reduce_scatter x1 -> x0, waiting for transfers between devices: 388 us -> none  [on_device(): lax.psum_scatter(full_table, ('gx', 'gy'), scatter_dimension=0, tiled=True)]
    dot_general x19 -> x0, matrix products: 146 us -> none  [the longest x10 95 us: apply_group(): jnp.einsum('rbq,bpq->rbp', charge_right[:, idx_second], tile, precision=h...]
    reduce_sum x11 -> x0, other arithmetic: 71.2 us -> none  [the longest x10 71.1 us: apply_group(): jnp.sum((pos_first[:, :, :, None] - pos_second[:, :, None, :]) ** 2, axis=0)]
    pallas_call x0 -> x2, Pallas kernels: none -> 67.7 us  [the longest x1 55.9 us: on_device(): pl.pallas_call(near_kernel, out_shape=[jax.ShapeDtypeStruct(shape, F32) f...]
    all_gather x1 -> x0, blocking collectives: 42.5 us -> none  [on_device(): table = lax.all_gather(proxies, ('gx', 'gy'), axis=1, tiled=True)]
    gather x53 -> x0, local copies, waits for them, and re-layouts: 25.3 us -> none  [the longest x20 6.07 us: apply_group(): pos_first = pos_left[:, idx_first]]
    scatter-add x18 -> x0, other arithmetic: 16.2 us -> none  [the longest x10 8.36 us: apply_group(): sum_left.at[:, idx_first]]
    reshape x6 -> x4, local copies, waits for them, and re-layouts: 16.8 us -> 1.04 us  [the longest x2 0.85 us: on_device(): proxies.reshape(3, CL_DEV, RANK).transpose(1, 0, 2)]
  transfers between devices with their start and end apart: 4 -> 0, of which waited for: 2 -> 0; matrix products, arithmetic and copies ran while one was open for 38% -> 0% of each run, Pallas kernels for 0% -> 0%
where the time goes in v1:
time: 74.7 us; the launch traced here: 74.4 us
  Pallas kernels  67.7 us (91%)
  local copies, waits for them, and re-layouts  5.61 us (8%)
  between operations  0.84 us (1%)
    pallas_call x1, Pallas kernels, on_device(): pl.pallas_call(near_kernel, out_shape=[jax.ShapeDtypeStruct(shape, F32) f...  55.9 us
    pallas_call x1, Pallas kernels, on_device(): pl.pallas_call(far_kernel, out_shape=jax.ShapeDtypeStruct((RHS, panels),...  11.8 us
    unnamed x12, local copies, waits for them, and re-layouts  2.66 us

profile of v1, /device:TPU:0, one launch (start us, length us, event | category | flops | bytes accessed | tf_op | source)
XLA Modules:
  0.0 74.4 jit_solution(1564022973953733071)
XLA Ops:
  0.0 0.0 copy-start
  0.8 0.7 slice_bitcast_fusion
  1.5 0.1 pad.12.clone
  1.5 0.8 %slice_reduce_fusion.1 = (s32[256]{0:T(256)S(1)}, s32[256]{0:T(256)S(1)}) fusion(s32[2,256]{1,0:T(2,128)} %param.17), kind=kLoop, calls=%fused_computation.12 | loop fusion | bytes 4096 | tf_op jit(solution)/shard_map/slice | solution.py:314
  2.3 0.1 fusion.3.cross_mask
  2.4 0.8 %reshape.31 = f32[3,32,16]{2,1,0:T(8,128)S(1)} reshape(f32[3,512]{1,0:T(4,128)} %param.13) | data formatting | bytes 12288 | tf_op jit(solution)/shard_map/reshape | solution.py:312
  3.2 0.1 copy.20
  3.2 0.1 copy.21
  3.3 0.2 reshape_squeeze.3
  3.5 0.1 squeeze.6
  3.6 0.1 add_add_fusion
  3.8 0.0 copy-start.2
  3.8 0.1 reshape.33
  3.9 0.1 reshape.34
  4.0 0.0 copy-start.4
  4.0 0.0 copy-start.5
  4.0 0.0 copy-done
  4.0 0.6 copy-done.2
  4.6 0.1 copy-done.4
  4.7 0.0 copy-done.5
  4.7 1.0 %copy-done.1 = f32[8,16384]{1,0:T(8,128)S(1)} copy-done((f32[8,16384]{1,0:T(8,128)S(1)}, f32[8,16384]{1,0:T(8,128)}, u32[]{:S(2)}) %copy-start.1) | copy-done | bytes 524312
  5.7 0.9 %copy-done.3 = f32[3,16384]{1,0:T(4,128)S(1)} copy-done((f32[3,16384]{1,0:T(4,128)S(1)}, f32[3,16384]{1,0:T(4,128)}, u32[]{:S(2)}) %copy-start.3) | copy-done | bytes 196632
  6.7 55.9 %shard_map.91 = (f32[8,16384]{1,0:T(8,128)S(1)}, f32[32,8,512]{2,1,0:T(8,128)S(1)}, f32[32,8,512]{2,1,0:T(8,128)S(1)}, f32[16,8,512]{2,1,0:T(8,128)S(1)}, f32[8,...) custom-call(f32[3,16384]{1,0:T(4,128)S(1)} %copy-done.3, f32[1,16384]{1,0:T(1,128)S(1)} %bitcast.9, ...), custom_call_target="tpu_custom_call" | custom-call | tf_op jit(solution)/shard_map/pallas_call | solution.py:328
  62.6 11.8 %shard_map.92 = f32[8,16384]{1,0:T(8,128)} custom-call(f32[1024,128]{1,0:T(8,128)S(1)} %bitcast.8, f32[32,128]{1,0:T(8,128)S(1)} %pad.4.proxy_table, f32[16,16384]{1,0:T(8,128)S(1)} %copy-done, f32[1,16384]{1,0:T(1,128)S(1)} %bitcast.10, f32[8,16384]{1,0:T(8,128)S(1)} %get-tuple-element.12.self_sum, f32[32,8,512]{2,1,0:T(8,128)S(1)} %get-tuple-element.13.first_sum, ...), custom_call_target="tpu_custom_call" | custom-call | tf_op jit(solution)/shard_map/pallas_call | solution.py:370
  (10 shorter events, 0.1 us)
Async XLA Ops:
  0.0 4.0 %copy-start = (f32[16,16384]{1,0:T(8,128)S(1)}, f32[16,16384]{1,0:T(8,128)}, u32[]{:S(2)}) copy-start(f32[16,16384]{1,0:T(8,128)} %basis.3) | copy-start | bytes 3145732
  3.8 0.8 %copy-start.2 = (f32[16384]{0:T(1024)S(1)}, f32[16384]{0:T(1024)}, u32[]{:S(2)}) copy-start(f32[16384]{0:T(1024)} %param.10) | copy-start | bytes 196612
  4.0 0.7 copy-start.4
  4.0 0.7 copy-start.5
  4.7 1.0 %copy-start.1 = (f32[8,16384]{1,0:T(8,128)S(1)}, f32[8,16384]{1,0:T(8,128)}, u32[]{:S(2)}) copy-start(f32[8,16384]{1,0:T(8,128)} %charges.1) | copy-start | bytes 1572868
  5.7 0.9 %copy-start.3 = (f32[3,16384]{1,0:T(4,128)S(1)}, f32[3,16384]{1,0:T(4,128)}, u32[]{:S(2)}) copy-start(f32[3,16384]{1,0:T(4,128)} %pos.1) | copy-start | bytes 589828

commit v2 on v1

v2 whole, which is shorter than its diff:
```python
import functools

import jax
import jax.numpy as jnp
from jax import lax
from jax.experimental import pallas as pl
from jax.experimental.pallas import tpu as pltpu
from jax.sharding import PartitionSpec as P

CLUSTER = 512
RANK = 16
RHS = 8
EDGE = 8
FOUR_PI_INV = 0.07957747154594767
SOFTENING = 0.0025
CL_DEV = 32
LOC_DEV = 32
CROSS_DEV = 16
PAIRS = CROSS_DEV + LOC_DEV
FAR_DEV = 256
EDGE_PANELS = EDGE * CLUSTER
CHUNK = 32
STRIP = 128
DEVICES = 128
N_Y, N_X, N_ZC = 4, 4, 8
ROWS = 8
MESH = pl.DeviceIdType.MESH
F32 = jnp.float32
BF16 = jnp.bfloat16


def dot(a, b, dims):
    return lax.dot_general(a, b, ((dims[:1], dims[1:]), ((), ())), preferred_element_type=F32)


def split(value, parts):
    out = []
    for _ in range(parts - 1):
        high = value.astype(BF16)
        out.append(high)
        value = value - high.astype(F32)
    out.append(value.astype(BF16))
    return out


def split_rows(value):
    high = value.astype(BF16).astype(F32)
    return jnp.concatenate([high, value - high], axis=0).astype(BF16)


def iotas(shape):
    return lax.broadcasted_iota(jnp.int32, shape, 0), lax.broadcasted_iota(jnp.int32, shape, 1)


def ones_where(condition):
    return jnp.where(condition, 1.0, 0.0).astype(BF16)


def cluster_cols(c):
    return slice(c * CLUSTER, (c + 1) * CLUSTER)


def near_kernel(
    pos_hbm, weight_hbm, charges_hbm, basis_hbm, proxies, far_blocks, cross_vector, local_pairs, cross_pairs, cross_count,
    self_sum, first_sum, second_sum, far_in, returned, info_in, proxy_table,
    pos, weight, charges, basis, cw, pos_c, pos_t, moments, coef_rows, proxy_rows, send, recv1, recv2, head_w, next_pos, next_w,
    info, hi0, hi1, lo0, lo1, load_sem, far_send, far_recv, far_own, edge_send, edge_recv,
):
    y = lax.axis_index("gx")
    gy = lax.axis_index("gy")
    x = gy // N_ZC
    zc = lax.rem(gy, N_ZC)
    flat = y * (N_X * N_ZC) + gy
    tile_hi, tile_lo = (hi0, hi1), (lo0, lo1)

    loads = [
        pltpu.make_async_copy(source, target, load_sem.at[i])
        for i, (source, target) in enumerate(
            ((weight_hbm, weight), (charges_hbm, charges), (pos_hbm, pos), (basis_hbm, basis))
        )
    ]
    for load in loads:
        load.start()

    def device_of(index):
        return (index // (N_X * N_ZC), lax.rem(index, N_X * N_ZC))

    after = device_of(lax.rem(flat + 1, DEVICES))
    before = device_of(lax.rem(flat + DEVICES - 1, DEVICES))
    peers = (
        [(lax.rem(y + i, N_Y), gy) for i in range(1, N_Y)]
        + [(y, lax.rem(x + i, N_X) * N_ZC + zc) for i in range(1, N_X)]
        + [(y, x * N_ZC + lax.rem(zc + i, N_ZC)) for i in range(1, N_ZC)]
    )
    barrier = pltpu.get_barrier_semaphore()
    for peer in peers + [after, before]:
        pl.semaphore_signal(barrier, inc=1, device_id=peer, device_id_type=MESH)

    info[...] = jnp.zeros_like(info)
    info[0:2, 0:CROSS_DEV] = cross_vector[...]
    info[2:3, :] = jnp.full((1, 128), cross_count[0], jnp.int32)

    columns = jnp.concatenate([proxies[...], jnp.zeros((5, CL_DEV * RANK), F32)], axis=0).T
    row, lane = iotas((CL_DEV * RANK, 128))
    spread = jnp.where(
        lane < RANK, columns[:, 0:1], jnp.where(lane < 2 * RANK, columns[:, 1:2], columns[:, 2:3])
    )
    spread = jnp.where((lax.rem(row, RANK) == lax.rem(lane, RANK)) & (lane < 3 * RANK), spread, 0.0)
    row, lane = iotas((CL_DEV, CL_DEV * RANK))
    gather = ones_where(row == lane // RANK)
    table = sum(dot(gather, part, (1, 0)) for part in split(spread, 3))
    proxy_table[...] = table

    for load in loads:
        load.wait()
    for c in range(CL_DEV):
        cols = cluster_cols(c)
        parts = split_rows(charges[:, cols] * weight[:, cols])
        cw[c] = parts
        place = jnp.concatenate([pos[:, cols], jnp.zeros((5, CLUSTER), F32)], axis=0)
        pos_c[c] = place
        pos_t[c] = place.T
        moments[c * 32 : (c + 1) * 32, :] = dot(split_rows(basis[:, cols]), parts, (1, 1))
    head_w[...] = charges[:, :EDGE_PANELS] * weight[:, :EDGE_PANELS]

    row, lane = iotas((2 * RHS, 128))
    spread = ones_where(lax.rem(row, RHS) == lax.rem(lane, RHS))
    wide = sum(dot(part, spread, (1, 0)) for part in split(moments[...], 3))
    row, lane = iotas(wide.shape)
    wide = jnp.where(lax.rem(row, RANK) == lane // RHS, wide, 0.0)
    coef = jnp.sum(wide.reshape(CL_DEV, 2 * RANK, 128), axis=1)

    row, lane = iotas((CL_DEV, 256))
    numbers = jnp.where(lane == 128 + 3 * RANK, row.astype(F32), 0.0).astype(BF16)
    both = jnp.concatenate(split(jnp.concatenate([coef, table], axis=1), 3) + [numbers], axis=0)
    row, lane = iotas((3 * CL_DEV, FAR_DEV))
    pick_source = jnp.where(lax.rem(row, CL_DEV) == far_blocks[0:1, :], 1.0, 0.0)
    row, lane = iotas((CL_DEV, FAR_DEV))
    pick_number = jnp.where(row == (far_blocks[1:2, :] & (CL_DEV - 1)), 1.0, 0.0)
    pick = jnp.concatenate([pick_source, pick_number], axis=0).astype(BF16)
    picked = dot(pick, both, (0, 0))
    coef_rows[...] = picked[:, :128]
    proxy_rows[...] = picked[:, 128:]
    for j in range(2):
        send[pl.ds(j, DEVICES, stride=ROWS), :] = coef_rows[pl.ds(j, DEVICES, stride=2), :]
        for k in range(2, ROWS, 2):
            send[pl.ds(k + j, DEVICES, stride=ROWS), :] = proxy_rows[pl.ds(j, DEVICES, stride=2), :]

    def far_copy(source, target, index, peer):
        return pltpu.make_async_remote_copy(
            src_ref=source, dst_ref=target, send_sem=far_send.at[index], recv_sem=far_recv.at[index],
            device_id=peer, device_id_type=MESH,
        )

    def edge_copy(source, target, index, peer):
        return pltpu.make_async_remote_copy(
            src_ref=source, dst_ref=target, send_sem=edge_send.at[index], recv_sem=edge_recv.at[index],
            device_id=peer, device_id_type=MESH,
        )

    def start(copies):
        for copy in copies:
            copy.start()

    def wait(copies):
        for copy in copies:
            copy.wait()

    def part(index, count):
        return pl.ds(pl.multiple_of(index * count, count), count)

    per_y, per_x = N_X * N_ZC * ROWS, N_ZC * ROWS
    phase1 = [pltpu.make_async_copy(send.at[part(y, per_y)], recv1.at[0], far_own.at[0])] + [
        far_copy(send.at[part(lax.rem(y + i, N_Y), per_y)], recv1.at[i], i - 1, peers[i - 1])
        for i in range(1, N_Y)
    ]
    phase2 = [pltpu.make_async_copy(recv1.at[:, part(x, per_x)], recv2.at[0], far_own.at[1])] + [
        far_copy(recv1.at[:, part(lax.rem(x + i, N_X), per_x)], recv2.at[i], 2 + i, peers[2 + i])
        for i in range(1, N_X)
    ]
    phase3 = [pltpu.make_async_copy(recv2.at[:, :, part(zc, ROWS)], far_in.at[0], far_own.at[2])] + [
        far_copy(recv2.at[:, :, part(lax.rem(zc + i, N_ZC), ROWS)], far_in.at[i], 5 + i, peers[5 + i])
        for i in range(1, N_ZC)
    ]
    heads = [
        edge_copy(pos.at[:, pl.ds(0, EDGE_PANELS)], next_pos, 0, before),
        edge_copy(head_w, next_w, 1, before),
        edge_copy(info, info_in, 2, after),
    ]
    give_back = [edge_copy(second_sum.at[pl.ds(0, CROSS_DEV)], returned, 3, after)]

    pl.semaphore_wait(barrier, len(peers) + 2)
    start(heads)
    start(phase1)

    def fill(row_cluster, columns, slot, row_from, row_to, col_from):
        col_x = columns[0:1, col_from:]
        col_y = columns[1:2, col_from:]
        col_z = columns[2:3, col_from:]
        for begin in range(row_from, row_to, CHUNK):
            rows = pos_t[row_cluster, begin : begin + CHUNK, :]
            dx = rows[:, 0:1] - col_x
            dy = rows[:, 1:2] - col_y
            dz = rows[:, 2:3] - col_z
            value = lax.rsqrt(dx * dx + dy * dy + dz * dz + SOFTENING)
            high = value.astype(BF16)
            tile_hi[slot][begin : begin + CHUNK, col_from:] = high
            tile_lo[slot][begin : begin + CHUNK, col_from:] = (value - high.astype(F32)).astype(BF16)

    def halves(parts, slot, rows, cols, side):
        sums = dot(parts, tile_hi[slot][rows, cols], (1, side)) + dot(parts, tile_lo[slot][rows, cols], (1, side))
        return sums[:RHS] + sums[RHS:]

    whole = slice(0, CLUSTER)

    def self_compute(t, slot):
        columns = pos_c[t]
        for begin in range(0, CLUSTER, STRIP):
            fill(t, columns, slot, begin, begin + STRIP, begin)

    def self_apply(t, slot):
        parts = cw[t]
        sums = [None] * (CLUSTER // STRIP)
        for i in range(CLUSTER // STRIP):
            rows = slice(i * STRIP, (i + 1) * STRIP)
            down = halves(parts[:, rows], slot, rows, slice(i * STRIP, CLUSTER), 0)
            for j in range(i, CLUSTER // STRIP):
                piece = down[:, (j - i) * STRIP : (j - i + 1) * STRIP]
                sums[j] = piece if sums[j] is None else sums[j] + piece
            if i + 1 < CLUSTER // STRIP:
                rest = slice((i + 1) * STRIP, CLUSTER)
                sums[i] = sums[i] + halves(parts[:, rest], slot, rows, rest, 1)
        self_sum[t] = jnp.concatenate(sums, axis=1)

    def pair_of(t):
        crossing = t < CROSS_DEV
        c, l = jnp.minimum(t, CROSS_DEV - 1), jnp.maximum(t - CROSS_DEV, 0)
        first = jnp.where(crossing, cross_pairs[0, c], local_pairs[0, l])
        second = jnp.where(crossing, cross_pairs[1, c] + CL_DEV, local_pairs[1, l])
        return first, second

    def pair_compute(t, slot):
        first, second = pair_of(t)
        fill(first, pos_c[second], slot, 0, CLUSTER, 0)

    def pair_apply(t, slot):
        first, second = pair_of(t)
        first_sum[t] = halves(cw[second], slot, whole, whole, 1)
        second_sum[t] = halves(cw[first], slot, whole, whole, 0)

    def section(count, compute, apply, middle, at):
        compute(0, 0)

        def body(i, carry):
            @pl.when(i == at)
            def _():
                middle()

            compute(2 * i + 1, 1)
            apply(2 * i, 0)
            compute(jnp.minimum(2 * i + 2, count - 1), 0)
            apply(2 * i + 1, 1)
            return carry

        lax.fori_loop(0, count // 2, body, 0)

    def self_middle():
        wait(phase1)
        start(phase2)

    section(CL_DEV, self_compute, self_apply, self_middle, CL_DEV // 4)
    wait(phase2)
    start(phase3)
    wait(heads)
    for j in range(EDGE):
        cw[CL_DEV + j] = split_rows(next_w[:, cluster_cols(j)])
        pos_c[CL_DEV + j, 0:3, :] = next_pos[:, cluster_cols(j)]
    section(PAIRS, pair_compute, pair_apply, lambda: start(give_back), CROSS_DEV // 2)
    wait(phase3)
    wait(give_back)


def far_kernel(
    far_in, proxy_table, basis, weight, self_sum, first_sum, second_sum, returned,
    local_pairs, cross_pairs, cross_count, info_in, out, near,
):
    def strided(j):
        return far_in[pl.ds(j, DEVICES, stride=ROWS), :]

    coef = jnp.concatenate([strided(0), strided(1)], axis=0)
    source = jnp.concatenate([strided(2), strided(3)], axis=0)
    row, lane = iotas((FAR_DEV, 128))
    number = jnp.sum(jnp.where(lane == 3 * RANK, source, 0.0), axis=1, keepdims=True).astype(jnp.int32)
    row, lane = iotas((FAR_DEV, CL_DEV))
    pick = ones_where(lane == number)
    target = sum(dot(pick, part, (1, 0)) for part in split(proxy_table[...], 3))
    row, lane = iotas((128, 3 * 256))
    axis = lane // 256
    from_target = ones_where(row == axis * RANK + lax.rem(lane, 256) // RANK)
    from_source = -ones_where(row == axis * RANK + lax.rem(lane, RANK))
    ends = split(target, 3) + split(source, 3)
    picks = [from_target] * 3 + [from_source] * 3
    offsets = sum(
        dot(jnp.concatenate(ends[i : i + 2], axis=1), jnp.concatenate(picks[i : i + 2], axis=0), (1, 0))
        for i in range(0, 6, 2)
    )
    offsets = offsets * offsets
    coupling = lax.rsqrt(offsets[:, :256] + offsets[:, 256:512] + offsets[:, 512:] + SOFTENING)
    coupling_parts = split(coupling, 2)
    coef_parts = jnp.concatenate(split(coef, 2), axis=1)
    contrib = jnp.zeros((FAR_DEV, 128), F32)
    row, lane = iotas((256, 256))
    half = lane // 128
    place = lax.rem(lane, 128)
    widen_from = row - (place // RHS) * RANK - half
    repeat_from = lax.rem(row, 128) - lax.rem(lane, RHS) - half * RHS
    for l in range(0, RANK, 2):
        widen = ones_where(widen_from == l)
        repeat = ones_where(repeat_from == l * RHS)
        left = dot(coupling_parts[0], widen, (1, 0)) + dot(coupling_parts[1], widen, (1, 0))
        product = left * dot(coef_parts, repeat, (1, 0))
        contrib = contrib + product[:, :128] + product[:, 128:]
    rowcoef = sum(dot(pick, part, (0, 0)) for part in split(contrib, 3))
    row, lane = iotas((CL_DEV * RHS, CL_DEV))
    eight = ones_where(row // RHS == lane)
    wide = sum(dot(eight, part, (1, 0)) for part in split(rowcoef, 3))
    row, lane = iotas(wide.shape)
    wide = jnp.where(lax.rem(row, RHS) == lax.rem(lane, RHS), wide, 0.0)
    row, lane = iotas((128, RANK))
    narrow = ones_where(row // RHS == lane)
    rows = sum(dot(part, narrow, (1, 0)) for part in split(wide, 3))
    rows_high = rows.astype(BF16).astype(F32)
    lefts = jnp.concatenate([rows_high, rows_high, rows - rows_high], axis=1)
    for c in range(CL_DEV):
        block = basis[:, cluster_cols(c)]
        high = block.astype(BF16).astype(F32)
        parts = jnp.concatenate([high, block - high, high], axis=0).astype(BF16)
        near[c] = self_sum[c] + dot(lefts[c * RHS : (c + 1) * RHS].astype(BF16), parts, (1, 0))

    def add_local(t, carry):
        near[local_pairs[0, t]] += first_sum[CROSS_DEV + t]
        near[local_pairs[1, t]] += second_sum[CROSS_DEV + t]
        return carry

    lax.fori_loop(0, LOC_DEV, add_local, 0)

    def add_cross(t, carry):
        near[cross_pairs[0, t]] += first_sum[t]
        return carry

    lax.fori_loop(0, cross_count[0], add_cross, 0)

    def add_returned(t, carry):
        near[info_in[1, t]] += returned[t]
        return carry

    lax.fori_loop(0, info_in[2, 0], add_returned, 0)
    for c in range(CL_DEV):
        cols = cluster_cols(c)
        out[:, cols] = near[c] * (weight[:, cols] * FOUR_PI_INV)


def on_device(
    positions, panel_weight, charges, basis, proxies, local_pairs, cross_pairs, cross_count, far_blocks
):
    panels = positions.shape[1]
    weight = panel_weight.reshape(1, panels)
    vmem = pl.BlockSpec(memory_space=pltpu.VMEM)
    smem = pl.BlockSpec(memory_space=pltpu.SMEM)
    hbm = pl.BlockSpec(memory_space=pltpu.HBM)

    def floats(*shape):
        return pltpu.VMEM(shape, F32)

    outs = pl.pallas_call(
        near_kernel,
        out_shape=[
            jax.ShapeDtypeStruct((CL_DEV, RHS, CLUSTER), F32),
            jax.ShapeDtypeStruct((PAIRS, RHS, CLUSTER), F32),
            jax.ShapeDtypeStruct((PAIRS, RHS, CLUSTER), F32),
            jax.ShapeDtypeStruct((N_ZC, N_X, N_Y, ROWS, 128), F32),
            jax.ShapeDtypeStruct((CROSS_DEV, RHS, CLUSTER), F32),
            jax.ShapeDtypeStruct((8, 128), jnp.int32),
            jax.ShapeDtypeStruct((CL_DEV, 128), F32),
        ],
        in_specs=[hbm] * 4 + [vmem] * 3 + [smem] * 3,
        out_specs=[vmem] * 7,
        scratch_shapes=[
            floats(3, panels),
            floats(1, panels),
            floats(RHS, panels),
            floats(RANK, panels),
            pltpu.VMEM((CL_DEV + EDGE, 2 * RHS, CLUSTER), BF16),
            floats(CL_DEV + EDGE, 8, CLUSTER),
            floats(CL_DEV, CLUSTER, 8),
            floats(CL_DEV * 2 * RANK, 2 * RHS),
            floats(FAR_DEV, 128),
            floats(FAR_DEV, 128),
            floats(DEVICES * ROWS, 128),
            floats(N_Y, N_X * N_ZC * ROWS, 128),
            floats(N_X, N_Y, N_ZC * ROWS, 128),
            floats(RHS, EDGE_PANELS),
            floats(3, EDGE_PANELS),
            floats(RHS, EDGE_PANELS),
            pltpu.VMEM((8, 128), jnp.int32),
        ]
        + [pltpu.VMEM((CLUSTER, CLUSTER), BF16)] * 4
        + [pltpu.SemaphoreType.DMA((count,)) for count in (4, 13, 13, 3, 4, 4)],
        compiler_params=pltpu.CompilerParams(
            collective_id=0, has_side_effects=True, vmem_limit_bytes=30 * 2**20
        ),
    )(
        positions, weight, charges, basis, proxies, far_blocks, cross_pairs, local_pairs, cross_pairs, cross_count
    )
    self_sum, first_sum, second_sum, far_in, returned, info_in, proxy_table = outs
    return pl.pallas_call(
        far_kernel,
        out_shape=jax.ShapeDtypeStruct((RHS, panels), F32),
        in_specs=[vmem] * 8 + [smem] * 4,
        out_specs=vmem,
        scratch_shapes=[floats(CL_DEV, RHS, CLUSTER)],
        compiler_params=pltpu.CompilerParams(vmem_limit_bytes=30 * 2**20),
    )(
        far_in.reshape(-1, 128), proxy_table, basis, weight, self_sum, first_sum, second_sum,
        returned, local_pairs, cross_pairs, cross_count, info_in,
    )


def solution(mesh):
    whole = P(None, ("gx", "gy"))
    flat = P(("gx", "gy"))
    return jax.shard_map(
        on_device,
        mesh=mesh,
        in_specs=(whole, flat, whole, whole, whole, whole, whole, flat, whole),
        out_specs=whole,
        check_vma=False,
    )
```

time: 74.7 us -> 64.5 us (0.86)
  Pallas kernels: 67.7 us -> 57.3 us
    pallas_call x1, Pallas kernels: 11.8 us -> 4.71 us  [on_device(): pl.pallas_call(far_kernel, out_shape=jax.ShapeDtypeStruct((RHS, panels),...]
    unnamed x12 -> x18, local copies, waits for them, and re-layouts: 2.66 us -> 6.1 us
    pallas_call x1, Pallas kernels: 55.9 us -> 52.6 us  [on_device(): pl.pallas_call(near_kernel, out_shape=[jax.ShapeDtypeStruct((CL_DEV, RHS,...]
    reshape x4 -> x0, local copies, waits for them, and re-layouts: 1.04 us -> none  [the longest x2 0.85 us: on_device(): proxies.reshape(3, CL_DEV, RANK).transpose(1, 0, 2)]
    slice x1 -> x0, local copies, waits for them, and re-layouts: 0.77 us -> none  [on_device(): source = far_blocks[0].reshape(DEVICES, 2)]
where the time goes in v2:
time: 64.5 us; the launch traced here: 64.1 us
  Pallas kernels  57.3 us (89%)
  local copies, waits for them, and re-layouts  6.1 us (9%)
  between operations  0.71 us (1%)
    pallas_call x1, Pallas kernels, on_device(): pl.pallas_call(near_kernel, out_shape=[jax.ShapeDtypeStruct((CL_DEV, RHS,...  52.6 us
    unnamed x18, local copies, waits for them, and re-layouts  6.1 us
    pallas_call x1, Pallas kernels, on_device(): pl.pallas_call(far_kernel, out_shape=jax.ShapeDtypeStruct((RHS, panels),...  4.71 us

profile of v2, /device:TPU:0, one launch (start us, length us, event | category | flops | bytes accessed | tf_op | source)
XLA Modules:
  0.0 64.1 jit_solution(11930963597935520466)
XLA Ops:
  0.0 0.0 copy-start.7
  0.7 0.0 copy-start.5
  0.7 0.0 copy-done.7
  0.7 0.7 %copy-done.5 = s32[2,16]{1,0:T(2,128)S(1)} copy-done((s32[2,16]{1,0:T(2,128)S(1)}, s32[2,16]{1,0:T(2,128)}, u32[]{:S(2)}) %copy-start.5) | copy-done | bytes 152
  1.3 0.0 copy-start
  1.4 1.2 %copy-done = f32[16,16384]{1,0:T(8,128)S(1)} copy-done((f32[16,16384]{1,0:T(8,128)S(1)}, f32[16,16384]{1,0:T(8,128)}, u32[]{:S(2)}) %copy-start) | copy-done | bytes 1048600
  2.6 0.0 copy-start.2
  2.6 1.0 %copy-done.2 = f32[8,16384]{1,0:T(8,128)S(1)} copy-done((f32[8,16384]{1,0:T(8,128)S(1)}, f32[8,16384]{1,0:T(8,128)}, u32[]{:S(2)}) %copy-start.2) | copy-done | bytes 524312
  3.6 0.0 copy-start.3
  3.6 0.8 %copy-done.3 = f32[16384]{0:T(1024)S(1)} copy-done((f32[16384]{0:T(1024)S(1)}, f32[16384]{0:T(1024)}, u32[]{:S(2)}) %copy-start.3) | copy-done | bytes 65560
  4.5 0.0 copy-start.4
  4.5 0.9 %copy-done.4 = f32[3,16384]{1,0:T(4,128)S(1)} copy-done((f32[3,16384]{1,0:T(4,128)S(1)}, f32[3,16384]{1,0:T(4,128)}, u32[]{:S(2)}) %copy-start.4) | copy-done | bytes 196632
  5.4 0.0 copy-start.6
  5.4 0.7 %copy-done.6 = f32[3,512]{1,0:T(4,128)S(1)} copy-done((f32[3,512]{1,0:T(4,128)S(1)}, f32[3,512]{1,0:T(4,128)}, u32[]{:S(2)}) %copy-start.6) | copy-done | bytes 6168
  6.1 0.0 copy-start.8
  6.1 0.7 %copy-done.8 = s32[2,256]{1,0:T(2,128)S(1)} copy-done((s32[2,256]{1,0:T(2,128)S(1)}, s32[2,256]{1,0:T(2,128)}, u32[]{:S(2)}) %copy-start.8) | copy-done | bytes 2072
  6.8 0.0 copy-start.1
  6.8 52.6 %shard_map.91 = (f32[32,8,512]{2,1,0:T(8,128)S(1)}, f32[48,8,512]{2,1,0:T(8,128)S(1)}, f32[48,8,512]{2,1,0:T(8,128)S(1)}, f32[8,4,4,8,128]{4,3,2,1,0:T(8,128)S(1...) custom-call(f32[3,16384]{1,0:T(4,128)S(1)} %copy-done.4, f32[1,16384]{1,0:T(1,128)S(1)} %bitcast.3, ...), custom_call_target="tpu_custom_call" | custom-call | tf_op jit(solution)/shard_map/pallas_call | solution.py:375
  59.4 0.0 copy-done.1
  59.4 4.7 %shard_map.92 = f32[8,16384]{1,0:T(8,128)} custom-call(f32[1024,128]{1,0:T(8,128)S(1)} %bitcast.2, f32[32,128]{1,0:T(8,128)S(1)} %get-tuple-element.13.proxy_table, f32[16,16384]{1,0:T(8,128)S(1)} %copy-done.1, f32[1,16384]{1,0:T(1,128)S(1)} %bitcast.4, f32[32,8,512]{2,1,0:T(8,128)S(1)} %get-tuple-element.14.self_sum, ...), custom_call_target="tpu_custom_call" | custom-call | tf_op jit(solution)/shard_map/pallas_call | solution.py:416
Async XLA Ops:
  0.0 0.7 %copy-start.7 = (s32[2,32]{1,0:T(2,128)S(1)}, s32[2,32]{1,0:T(2,128)}, u32[]{:S(2)}) copy-start(s32[2,32]{1,0:T(2,128)} %local_pairs.3) | copy-start | bytes 772
  0.7 0.7 %copy-start.5 = (s32[2,16]{1,0:T(2,128)S(1)}, s32[2,16]{1,0:T(2,128)}, u32[]{:S(2)}) copy-start(s32[2,16]{1,0:T(2,128)} %cross_pairs.3) | copy-start | bytes 388
  1.3 1.2 %copy-start = (f32[16,16384]{1,0:T(8,128)S(1)}, f32[16,16384]{1,0:T(8,128)}, u32[]{:S(2)}) copy-start(f32[16,16384]{1,0:T(8,128)} %basis.1) | copy-start | bytes 3145732
  2.6 1.0 %copy-start.2 = (f32[8,16384]{1,0:T(8,128)S(1)}, f32[8,16384]{1,0:T(8,128)}, u32[]{:S(2)}) copy-start(f32[8,16384]{1,0:T(8,128)} %charges_hbm.1) | copy-start | bytes 1572868
  3.6 0.8 %copy-start.3 = (f32[16384]{0:T(1024)S(1)}, f32[16384]{0:T(1024)}, u32[]{:S(2)}) copy-start(f32[16384]{0:T(1024)} %param.10) | copy-start | bytes 196612
  4.5 0.9 %copy-start.4 = (f32[3,16384]{1,0:T(4,128)S(1)}, f32[3,16384]{1,0:T(4,128)}, u32[]{:S(2)}) copy-start(f32[3,16384]{1,0:T(4,128)} %pos_hbm.1) | copy-start | bytes 589828
  5.4 0.7 %copy-start.6 = (f32[3,512]{1,0:T(4,128)S(1)}, f32[3,512]{1,0:T(4,128)}, u32[]{:S(2)}) copy-start(f32[3,512]{1,0:T(4,128)} %proxies.1) | copy-start | bytes 18436
  6.1 0.7 %copy-start.8 = (s32[2,256]{1,0:T(2,128)S(1)}, s32[2,256]{1,0:T(2,128)}, u32[]{:S(2)}) copy-start(s32[2,256]{1,0:T(2,128)} %far_blocks.1) | copy-start | bytes 6148
  6.8 52.6 %copy-start.1 = (f32[16,16384]{1,0:T(8,128)S(1)}, f32[16,16384]{1,0:T(8,128)}, u32[]{:S(2)}) copy-start(f32[16,16384]{1,0:T(8,128)} %basis.1) | copy-start | bytes 3145732

commit v3 on v2

--- a/solution.py
+++ b/solution.py
@@ -17,6 +17,7 @@
 LOC_DEV = 32
 CROSS_DEV = 16
 PAIRS = CROSS_DEV + LOC_DEV
+EARLY = 8
 FAR_DEV = 256
 EDGE_PANELS = EDGE * CLUSTER
 CHUNK = 32
@@ -62,9 +63,9 @@
 
 def near_kernel(
     pos_hbm, weight_hbm, charges_hbm, basis_hbm, proxies, far_blocks, cross_vector, local_pairs, cross_pairs, cross_count,
-    self_sum, first_sum, second_sum, far_in, returned, info_in, proxy_table,
-    pos, weight, charges, basis, cw, pos_c, pos_t, moments, coef_rows, proxy_rows, send, recv1, recv2, head_w, next_pos, next_w,
-    info, hi0, hi1, lo0, lo1, load_sem, far_send, far_recv, far_own, edge_send, edge_recv,
+    self_out, first_out, second_out, far_in, returned, info_in, proxy_table,
+    self_sum, first_sum, second_sum, pos, weight, charges, basis, cw, pos_c, pos_t, moments, coef_rows, proxy_rows, send, recv1, recv2, head_w, next_pos, next_w,
+    info, hi0, hi1, lo0, lo1, load_sem, far_send, far_recv, far_own, edge_send, edge_recv, out_sem,
 ):
     y = lax.axis_index("gx")
     gy = lax.axis_index("gy")
@@ -187,11 +188,22 @@
         edge_copy(head_w, next_w, 1, before),
         edge_copy(info, info_in, 2, after),
     ]
-    give_back = [edge_copy(second_sum.at[pl.ds(0, CROSS_DEV)], returned, 3, after)]
-
-    pl.semaphore_wait(barrier, len(peers) + 2)
-    start(heads)
-    start(phase1)
+    crossing = pl.ds(EARLY, CROSS_DEV)
+    give_back = [edge_copy(second_sum.at[crossing], returned, 3, after)]
+
+    def out_copies(index, first, count, *pairs):
+        rows = pl.ds(first, count)
+        return [
+            pltpu.make_async_copy(source.at[rows], target.at[rows], out_sem.at[index + i])
+            for i, (source, target) in enumerate(pairs)
+        ]
+
+    first_pair, second_pair = (first_sum, first_out), (second_sum, second_out)
+    done = EARLY + CROSS_DEV
+    outs_self = out_copies(0, 0, CL_DEV, (self_sum, self_out))
+    outs_early = out_copies(1, 0, done, first_pair) + out_copies(2, 0, EARLY, second_pair)
+    outs_late = out_copies(3, done, 16, first_pair, second_pair)
+    outs_last = out_copies(5, done + 16, 8, first_pair, second_pair)
 
     def fill(row_cluster, columns, slot, row_from, row_to, col_from):
         col_x = columns[0:1, col_from:]
@@ -233,10 +245,11 @@
         self_sum[t] = jnp.concatenate(sums, axis=1)
 
     def pair_of(t):
-        crossing = t < CROSS_DEV
-        c, l = jnp.minimum(t, CROSS_DEV - 1), jnp.maximum(t - CROSS_DEV, 0)
-        first = jnp.where(crossing, cross_pairs[0, c], local_pairs[0, l])
-        second = jnp.where(crossing, cross_pairs[1, c] + CL_DEV, local_pairs[1, l])
+        crosses = (t >= EARLY) & (t < done)
+        c = jnp.clip(t - EARLY, 0, CROSS_DEV - 1)
+        l = jnp.clip(jnp.where(t < EARLY, t, t - CROSS_DEV), 0, LOC_DEV - 1)
+        first = jnp.where(crosses, cross_pairs[0, c], local_pairs[0, l])
+        second = jnp.where(crosses, cross_pairs[1, c] + CL_DEV, local_pairs[1, l])
         return first, second
 
     def pair_compute(t, slot):
@@ -248,14 +261,12 @@
         first_sum[t] = halves(cw[second], slot, whole, whole, 1)
         second_sum[t] = halves(cw[first], slot, whole, whole, 0)
 
-    def section(count, compute, apply, middle, at):
+    def section(count, compute, apply, steps):
         compute(0, 0)
 
         def body(i, carry):
-            @pl.when(i == at)
-            def _():
-                middle()
-
+            for at, step in steps:
+                pl.when(i == at)(step)
             compute(2 * i + 1, 1)
             apply(2 * i, 0)
             compute(jnp.minimum(2 * i + 2, count - 1), 0)
@@ -264,26 +275,67 @@
 
         lax.fori_loop(0, count // 2, body, 0)
 
-    def self_middle():
-        wait(phase1)
-        start(phase2)
-
-    section(CL_DEV, self_compute, self_apply, self_middle, CL_DEV // 4)
-    wait(phase2)
-    start(phase3)
-    wait(heads)
-    for j in range(EDGE):
-        cw[CL_DEV + j] = split_rows(next_w[:, cluster_cols(j)])
-        pos_c[CL_DEV + j, 0:3, :] = next_pos[:, cluster_cols(j)]
-    section(PAIRS, pair_compute, pair_apply, lambda: start(give_back), CROSS_DEV // 2)
+    def send_first():
+        pl.semaphore_wait(barrier, len(peers) + 2)
+        start(heads)
+        start(phase1)
+
+    def take_heads():
+        wait(heads)
+        for j in range(EDGE):
+            cw[CL_DEV + j] = split_rows(next_w[:, cluster_cols(j)])
+            pos_c[CL_DEV + j, 0:3, :] = next_pos[:, cluster_cols(j)]
+
+    def send_last():
+        wait(phase2)
+        start(phase3)
+
+    def send_back():
+        start(give_back)
+        start(outs_early)
+
+    section(CL_DEV, self_compute, self_apply, [(2, send_first)])
+    start(outs_self)
+    wait(phase1)
+    start(phase2)
+    section(
+        PAIRS,
+        pair_compute,
+        pair_apply,
+        [(EARLY // 2 - 1, take_heads), (10, send_last), (done // 2, send_back), (done // 2 + 8, lambda: start(outs_late))],
+    )
+    start(outs_last)
+    wait(outs_self)
+    wait(outs_early)
+    wait(outs_late)
     wait(phase3)
     wait(give_back)
+    wait(outs_last)
 
 
 def far_kernel(
-    far_in, proxy_table, basis, weight, self_sum, first_sum, second_sum, returned,
-    local_pairs, cross_pairs, cross_count, info_in, out, near,
+    far_hbm, proxy_table, basis_hbm, weight_hbm, self_hbm, first_hbm, second_hbm, returned_hbm,
+    local_pairs, cross_pairs, cross_count, info_in,
+    out, near, far_in, basis, weight, self_sum, first_sum, second_sum, returned, load_sem,
 ):
+    loads = [
+        pltpu.make_async_copy(source, target, load_sem.at[i])
+        for i, (source, target) in enumerate(
+            (
+                (far_hbm, far_in),
+                (basis_hbm, basis),
+                (self_hbm, self_sum),
+                (first_hbm, first_sum),
+                (second_hbm, second_sum),
+                (returned_hbm, returned),
+                (weight_hbm, weight),
+            )
+        )
+    ]
+    for load in loads:
+        load.start()
+    loads[0].wait()
+
     def strided(j):
         return far_in[pl.ds(j, DEVICES, stride=ROWS), :]
 
@@ -331,6 +383,8 @@
     rows = sum(dot(part, narrow, (1, 0)) for part in split(wide, 3))
     rows_high = rows.astype(BF16).astype(F32)
     lefts = jnp.concatenate([rows_high, rows_high, rows - rows_high], axis=1)
+    for load in loads[1:]:
+        load.wait()
     for c in range(CL_DEV):
         block = basis[:, cluster_cols(c)]
         high = block.astype(BF16).astype(F32)
@@ -338,14 +392,15 @@
         near[c] = self_sum[c] + dot(lefts[c * RHS : (c + 1) * RHS].astype(BF16), parts, (1, 0))
 
     def add_local(t, carry):
-        near[local_pairs[0, t]] += first_sum[CROSS_DEV + t]
-        near[local_pairs[1, t]] += second_sum[CROSS_DEV + t]
+        slot = jnp.where(t < EARLY, t, t + CROSS_DEV)
+        near[local_pairs[0, t]] += first_sum[slot]
+        near[local_pairs[1, t]] += second_sum[slot]
         return carry
 
     lax.fori_loop(0, LOC_DEV, add_local, 0)
 
     def add_cross(t, carry):
-        near[cross_pairs[0, t]] += first_sum[t]
+        near[cross_pairs[0, t]] += first_sum[EARLY + t]
         return carry
 
     lax.fori_loop(0, cross_count[0], add_cross, 0)
@@ -384,8 +439,11 @@
             jax.ShapeDtypeStruct((CL_DEV, 128), F32),
         ],
         in_specs=[hbm] * 4 + [vmem] * 3 + [smem] * 3,
-        out_specs=[vmem] * 7,
+        out_specs=[hbm] * 6 + [vmem],
         scratch_shapes=[
+            floats(CL_DEV, RHS, CLUSTER),
+            floats(PAIRS, RHS, CLUSTER),
+            floats(PAIRS, RHS, CLUSTER),
             floats(3, panels),
             floats(1, panels),
             floats(RHS, panels),
@@ -405,9 +463,9 @@
             pltpu.VMEM((8, 128), jnp.int32),
         ]
         + [pltpu.VMEM((CLUSTER, CLUSTER), BF16)] * 4
-        + [pltpu.SemaphoreType.DMA((count,)) for count in (4, 13, 13, 3, 4, 4)],
+        + [pltpu.SemaphoreType.DMA((count,)) for count in (4, 13, 13, 3, 4, 4, 7)],
         compiler_params=pltpu.CompilerParams(
-            collective_id=0, has_side_effects=True, vmem_limit_bytes=30 * 2**20
+            collective_id=0, has_side_effects=True, vmem_limit_bytes=60 * 2**20
         ),
     )(
         positions, weight, charges, basis, proxies, far_blocks, cross_pairs, local_pairs, cross_pairs, cross_count
@@ -416,10 +474,20 @@
     return pl.pallas_call(
         far_kernel,
         out_shape=jax.ShapeDtypeStruct((RHS, panels), F32),
-        in_specs=[vmem] * 8 + [smem] * 4,
+        in_specs=[hbm, vmem] + [hbm] * 6 + [smem] * 4,
         out_specs=vmem,
-        scratch_shapes=[floats(CL_DEV, RHS, CLUSTER)],
-        compiler_params=pltpu.CompilerParams(vmem_limit_bytes=30 * 2**20),
+        scratch_shapes=[
+            floats(CL_DEV, RHS, CLUSTER),
+            floats(DEVICES * ROWS, 128),
+            floats(RANK, panels),
+            floats(1, panels),
+            floats(CL_DEV, RHS, CLUSTER),
+            floats(PAIRS, RHS, CLUSTER),
+            floats(PAIRS, RHS, CLUSTER),
+            floats(CROSS_DEV, RHS, CLUSTER),
+            pltpu.SemaphoreType.DMA((7,)),
+        ],
+        compiler_params=pltpu.CompilerParams(vmem_limit_bytes=60 * 2**20),
     )(
         far_in.reshape(-1, 128), proxy_table, basis, weight, self_sum, first_sum, second_sum,
         returned, local_pairs, cross_pairs, cross_count, info_in,

time: 64.5 us -> 56.5 us (0.88)
  local copies, waits for them, and re-layouts: 6.1 us -> 0 us
  Pallas kernels: 57.3 us -> 55.6 us
    unnamed x18 -> x0, local copies, waits for them, and re-layouts: 6.1 us -> none
    pallas_call x1, Pallas kernels: 52.6 us -> 49.4 us  [on_device(): pl.pallas_call(near_kernel, out_shape=[jax.ShapeDtypeStruct((CL_DEV, RHS,...]
    pallas_call x1, Pallas kernels: 4.71 us -> 6.18 us  [on_device(): pl.pallas_call(far_kernel, out_shape=jax.ShapeDtypeStruct((RHS, panels),...]
where the time goes in v3:
time: 56.5 us; the launch traced here: 56.2 us
  Pallas kernels  55.6 us (98%)
  between operations  0.66 us (1%)
    pallas_call x1, Pallas kernels, on_device(): pl.pallas_call(near_kernel, out_shape=[jax.ShapeDtypeStruct((CL_DEV, RHS,...  49.4 us
    pallas_call x1, Pallas kernels, on_device(): pl.pallas_call(far_kernel, out_shape=jax.ShapeDtypeStruct((RHS, panels),...  6.18 us

profile of v3, /device:TPU:0, one launch (start us, length us, event | category | flops | bytes accessed | tf_op | source)
XLA Modules:
  0.0 56.2 jit_solution(15359791965820772135)
XLA Ops:
  0.7 49.4 %shard_map.91 = (f32[32,8,512]{2,1,0:T(8,128)}, f32[48,8,512]{2,1,0:T(8,128)}, f32[48,8,512]{2,1,0:T(8,128)}, f32[8,4,4,8,128]{4,3,2,1,0:T(8,128)}, f32[16,8,512...) custom-call(f32[3,16384]{1,0:T(4,128)} %pos_hbm.1, f32[1,16384]{1,0:T(1,128)} %bitcast.3, f32[8,16384]{1,0:T(8,128)} %charges_hbm.1, ...), custom_call_target="tpu_custom_call" | custom-call | tf_op jit(solution)/shard_map/pallas_call | solution.py:430
  50.0 6.2 %shard_map.92 = f32[8,16384]{1,0:T(8,128)} custom-call(f32[1024,128]{1,0:T(8,128)} %bitcast.2, f32[32,128]{1,0:T(8,128)} %get-tuple-element.13.proxy_table, f32[16,16384]{1,0:T(8,128)} %basis_hbm.3, f32[1,16384]{1,0:T(1,128)} %bitcast.4, f32[32,8,512]{2,1,0:T(8,128)} %get-tuple-element.14.self_hbm, f32[48,8,512]{2,1,0:T(8,128)} %get-tuple-element.15.first_hbm, ...), custom_call_target="tpu_custom_call" | custom-call | tf_op jit(solution)/shard_map/pallas_call | solution.py:474

commit v4 on v3

--- a/solution.py
+++ b/solution.py
@@ -20,7 +20,8 @@
 EARLY = 8
 FAR_DEV = 256
 EDGE_PANELS = EDGE * CLUSTER
-CHUNK = 32
+SELF_CHUNK = 32
+PAIR_CHUNK = 16
 STRIP = 128
 DEVICES = 128
 N_Y, N_X, N_ZC = 4, 4, 8
@@ -205,19 +206,19 @@
     outs_late = out_copies(3, done, 16, first_pair, second_pair)
     outs_last = out_copies(5, done + 16, 8, first_pair, second_pair)
 
-    def fill(row_cluster, columns, slot, row_from, row_to, col_from):
+    def fill(row_cluster, columns, slot, row_from, row_to, col_from, chunk):
         col_x = columns[0:1, col_from:]
         col_y = columns[1:2, col_from:]
         col_z = columns[2:3, col_from:]
-        for begin in range(row_from, row_to, CHUNK):
-            rows = pos_t[row_cluster, begin : begin + CHUNK, :]
+        for begin in range(row_from, row_to, chunk):
+            rows = pos_t[row_cluster, begin : begin + chunk, :]
             dx = rows[:, 0:1] - col_x
             dy = rows[:, 1:2] - col_y
             dz = rows[:, 2:3] - col_z
             value = lax.rsqrt(dx * dx + dy * dy + dz * dz + SOFTENING)
             high = value.astype(BF16)
-            tile_hi[slot][begin : begin + CHUNK, col_from:] = high
-            tile_lo[slot][begin : begin + CHUNK, col_from:] = (value - high.astype(F32)).astype(BF16)
+            tile_hi[slot][begin : begin + chunk, col_from:] = high
+            tile_lo[slot][begin : begin + chunk, col_from:] = (value - high.astype(F32)).astype(BF16)
 
     def halves(parts, slot, rows, cols, side):
         sums = dot(parts, tile_hi[slot][rows, cols], (1, side)) + dot(parts, tile_lo[slot][rows, cols], (1, side))
@@ -228,7 +229,7 @@
     def self_compute(t, slot):
         columns = pos_c[t]
         for begin in range(0, CLUSTER, STRIP):
-            fill(t, columns, slot, begin, begin + STRIP, begin)
+            fill(t, columns, slot, begin, begin + STRIP, begin, SELF_CHUNK)
 
     def self_apply(t, slot):
         parts = cw[t]
@@ -254,7 +255,7 @@
 
     def pair_compute(t, slot):
         first, second = pair_of(t)
-        fill(first, pos_c[second], slot, 0, CLUSTER, 0)
+        fill(first, pos_c[second], slot, 0, CLUSTER, 0, PAIR_CHUNK)
 
     def pair_apply(t, slot):
         first, second = pair_of(t)
@@ -316,7 +317,7 @@
 def far_kernel(
     far_hbm, proxy_table, basis_hbm, weight_hbm, self_hbm, first_hbm, second_hbm, returned_hbm,
     local_pairs, cross_pairs, cross_count, info_in,
-    out, near, far_in, basis, weight, self_sum, first_sum, second_sum, returned, load_sem,
+    out, near, far_in, basis, weight, self_sum, first_sum, second_sum, returned, coef, target, coupling, contrib, load_sem,
 ):
     loads = [
         pltpu.make_async_copy(source, target, load_sem.at[i])
@@ -339,40 +340,27 @@
     def strided(j):
         return far_in[pl.ds(j, DEVICES, stride=ROWS), :]
 
-    coef = jnp.concatenate([strided(0), strided(1)], axis=0)
-    source = jnp.concatenate([strided(2), strided(3)], axis=0)
-    row, lane = iotas((FAR_DEV, 128))
-    number = jnp.sum(jnp.where(lane == 3 * RANK, source, 0.0), axis=1, keepdims=True).astype(jnp.int32)
-    row, lane = iotas((FAR_DEV, CL_DEV))
-    pick = ones_where(lane == number)
-    target = sum(dot(pick, part, (1, 0)) for part in split(proxy_table[...], 3))
-    row, lane = iotas((128, 3 * 256))
-    axis = lane // 256
-    from_target = ones_where(row == axis * RANK + lax.rem(lane, 256) // RANK)
-    from_source = -ones_where(row == axis * RANK + lax.rem(lane, RANK))
-    ends = split(target, 3) + split(source, 3)
-    picks = [from_target] * 3 + [from_source] * 3
-    offsets = sum(
-        dot(jnp.concatenate(ends[i : i + 2], axis=1), jnp.concatenate(picks[i : i + 2], axis=0), (1, 0))
-        for i in range(0, 6, 2)
-    )
-    offsets = offsets * offsets
-    coupling = lax.rsqrt(offsets[:, :256] + offsets[:, 256:512] + offsets[:, 512:] + SOFTENING)
-    coupling_parts = split(coupling, 2)
-    coef_parts = jnp.concatenate(split(coef, 2), axis=1)
-    contrib = jnp.zeros((FAR_DEV, 128), F32)
-    row, lane = iotas((256, 256))
-    half = lane // 128
-    place = lax.rem(lane, 128)
-    widen_from = row - (place // RHS) * RANK - half
-    repeat_from = lax.rem(row, 128) - lax.rem(lane, RHS) - half * RHS
-    for l in range(0, RANK, 2):
-        widen = ones_where(widen_from == l)
-        repeat = ones_where(repeat_from == l * RHS)
-        left = dot(coupling_parts[0], widen, (1, 0)) + dot(coupling_parts[1], widen, (1, 0))
-        product = left * dot(coef_parts, repeat, (1, 0))
-        contrib = contrib + product[:, :128] + product[:, 128:]
-    rowcoef = sum(dot(pick, part, (0, 0)) for part in split(contrib, 3))
+    coef[...] = jnp.concatenate([strided(0).T, strided(1).T], axis=1)
+    source = jnp.concatenate([strided(2).T, strided(3).T], axis=1)
+    number = source[3 * RANK : 3 * RANK + 1, :].astype(jnp.int32)
+    row, lane = iotas((CL_DEV, FAR_DEV))
+    pick = ones_where(row == number)
+    target[...] = sum(dot(part, pick, (0, 0)) for part in split(proxy_table[...], 3))
+    for k in range(RANK):
+        distance = SOFTENING
+        for axis in range(3):
+            end = axis * RANK + k
+            offset = target[end : end + 1, :] - source[axis * RANK : (axis + 1) * RANK, :]
+            distance = distance + offset * offset
+        coupling[k * RANK : (k + 1) * RANK, :] = lax.rsqrt(distance)
+    for k in range(RANK):
+        total = None
+        for l in range(RANK):
+            entry = k * RANK + l
+            term = coupling[entry : entry + 1, :] * coef[l * RHS : (l + 1) * RHS, :]
+            total = term if total is None else total + term
+        contrib[k * RHS : (k + 1) * RHS, :] = total
+    rowcoef = sum(dot(pick, part, (1, 1)) for part in split(contrib[...], 3))
     row, lane = iotas((CL_DEV * RHS, CL_DEV))
     eight = ones_where(row // RHS == lane)
     wide = sum(dot(eight, part, (1, 0)) for part in split(rowcoef, 3))
@@ -485,6 +473,10 @@
             floats(PAIRS, RHS, CLUSTER),
             floats(PAIRS, RHS, CLUSTER),
             floats(CROSS_DEV, RHS, CLUSTER),
+            floats(128, FAR_DEV),
+            floats(128, FAR_DEV),
+            floats(RANK * RANK, FAR_DEV),
+            floats(128, FAR_DEV),
             pltpu.SemaphoreType.DMA((7,)),
         ],
         compiler_params=pltpu.CompilerParams(vmem_limit_bytes=60 * 2**20),

time: 56.5 us -> 54.3 us (0.961)
  Pallas kernels: 55.6 us -> 53.4 us
    pallas_call x1, Pallas kernels: 6.18 us -> 4.83 us  [on_device(): pl.pallas_call(far_kernel, out_shape=jax.ShapeDtypeStruct((RHS, panels),...]
    pallas_call x1, Pallas kernels: 49.4 us -> 48.6 us  [on_device(): pl.pallas_call(near_kernel, out_shape=[jax.ShapeDtypeStruct((CL_DEV, RHS,...]
where the time goes in v4:
time: 54.3 us; the launch traced here: 54.1 us
  Pallas kernels  53.4 us (98%)
  between operations  0.66 us (1%)
    pallas_call x1, Pallas kernels, on_device(): pl.pallas_call(near_kernel, out_shape=[jax.ShapeDtypeStruct((CL_DEV, RHS,...  48.6 us
    pallas_call x1, Pallas kernels, on_device(): pl.pallas_call(far_kernel, out_shape=jax.ShapeDtypeStruct((RHS, panels),...  4.83 us

profile of v4, /device:TPU:0, one launch (start us, length us, event | category | flops | bytes accessed | tf_op | source)
XLA Modules:
  0.0 54.1 jit_solution(2041363120259052144)
XLA Ops:
  0.7 48.6 %shard_map.91 = (f32[32,8,512]{2,1,0:T(8,128)}, f32[48,8,512]{2,1,0:T(8,128)}, f32[48,8,512]{2,1,0:T(8,128)}, f32[8,4,4,8,128]{4,3,2,1,0:T(8,128)}, f32[16,8,512...) custom-call(f32[3,16384]{1,0:T(4,128)} %pos_hbm.1, f32[1,16384]{1,0:T(1,128)} %bitcast.3, f32[8,16384]{1,0:T(8,128)} %charges_hbm.1, ...), custom_call_target="tpu_custom_call" | custom-call | tf_op jit(solution)/shard_map/pallas_call | solution.py:418
  49.3 4.8 %shard_map.92 = f32[8,16384]{1,0:T(8,128)} custom-call(f32[1024,128]{1,0:T(8,128)} %bitcast.2, f32[32,128]{1,0:T(8,128)} %get-tuple-element.13.proxy_table, f32[16,16384]{1,0:T(8,128)} %basis_hbm.3, f32[1,16384]{1,0:T(1,128)} %bitcast.4, f32[32,8,512]{2,1,0:T(8,128)} %get-tuple-element.14.self_hbm, f32[48,8,512]{2,1,0:T(8,128)} %get-tuple-element.15.first_hbm, ...), custom_call_target="tpu_custom_call" | custom-call | tf_op jit(solution)/shard_map/pallas_call | solution.py:462

commit v5 on v4

--- a/solution.py
+++ b/solution.py
@@ -65,7 +65,7 @@
 def near_kernel(
     pos_hbm, weight_hbm, charges_hbm, basis_hbm, proxies, far_blocks, cross_vector, local_pairs, cross_pairs, cross_count,
     self_out, first_out, second_out, far_in, returned, info_in, proxy_table,
-    self_sum, first_sum, second_sum, pos, weight, charges, basis, cw, pos_c, pos_t, moments, coef_rows, proxy_rows, send, recv1, recv2, head_w, next_pos, next_w,
+    self_sum, first_sum, second_sum, pos, weight, charges, basis, cw, pos_c, pos_t, moments, coef_rows, proxy_rows, send, recv, head_w, next_pos, next_w,
     info, hi0, hi1, lo0, lo1, load_sem, far_send, far_recv, far_own, edge_send, edge_recv, out_sem,
 ):
     y = lax.axis_index("gx")
@@ -89,11 +89,10 @@
 
     after = device_of(lax.rem(flat + 1, DEVICES))
     before = device_of(lax.rem(flat + DEVICES - 1, DEVICES))
-    peers = (
-        [(lax.rem(y + i, N_Y), gy) for i in range(1, N_Y)]
-        + [(y, lax.rem(x + i, N_X) * N_ZC + zc) for i in range(1, N_X)]
-        + [(y, x * N_ZC + lax.rem(zc + i, N_ZC)) for i in range(1, N_ZC)]
-    )
+    chips = [(lax.rem(y + i // N_X, N_Y), lax.rem(x + i % N_X, N_X)) for i in range(1, N_Y * N_X)]
+    peers = [(to_y, to_x * N_ZC + zc) for to_y, to_x in chips] + [
+        (y, x * N_ZC + lax.rem(zc + i, N_ZC)) for i in range(1, N_ZC)
+    ]
     barrier = pltpu.get_barrier_semaphore()
     for peer in peers + [after, before]:
         pl.semaphore_signal(barrier, inc=1, device_id=peer, device_id_type=MESH)
@@ -171,17 +170,13 @@
     def part(index, count):
         return pl.ds(pl.multiple_of(index * count, count), count)
 
-    per_y, per_x = N_X * N_ZC * ROWS, N_ZC * ROWS
-    phase1 = [pltpu.make_async_copy(send.at[part(y, per_y)], recv1.at[0], far_own.at[0])] + [
-        far_copy(send.at[part(lax.rem(y + i, N_Y), per_y)], recv1.at[i], i - 1, peers[i - 1])
-        for i in range(1, N_Y)
-    ]
-    phase2 = [pltpu.make_async_copy(recv1.at[:, part(x, per_x)], recv2.at[0], far_own.at[1])] + [
-        far_copy(recv1.at[:, part(lax.rem(x + i, N_X), per_x)], recv2.at[i], 2 + i, peers[2 + i])
-        for i in range(1, N_X)
-    ]
-    phase3 = [pltpu.make_async_copy(recv2.at[:, :, part(zc, ROWS)], far_in.at[0], far_own.at[2])] + [
-        far_copy(recv2.at[:, :, part(lax.rem(zc + i, N_ZC), ROWS)], far_in.at[i], 5 + i, peers[5 + i])
+    per_chip = N_ZC * ROWS
+    phase1 = [pltpu.make_async_copy(send.at[part(y * N_X + x, per_chip)], recv.at[0], far_own.at[0])] + [
+        far_copy(send.at[part(to_y * N_X + to_x, per_chip)], recv.at[i + 1], i, peers[i])
+        for i, (to_y, to_x) in enumerate(chips)
+    ]
+    phase2 = [pltpu.make_async_copy(recv.at[:, part(zc, ROWS)], far_in.at[0], far_own.at[1])] + [
+        far_copy(recv.at[:, part(lax.rem(zc + i, N_ZC), ROWS)], far_in.at[i], len(chips) + i - 1, peers[len(chips) + i - 1])
         for i in range(1, N_ZC)
     ]
     heads = [
@@ -190,7 +185,8 @@
         edge_copy(info, info_in, 2, after),
     ]
     crossing = pl.ds(EARLY, CROSS_DEV)
-    give_back = [edge_copy(second_sum.at[crossing], returned, 3, after)]
+    give_back = edge_copy(second_sum.at[crossing], returned, 3, after)
+    gives, gets = flat < DEVICES - 1, flat > 0
 
     def out_copies(index, first, count, *pairs):
         rows = pl.ds(first, count)
@@ -207,9 +203,9 @@
     outs_last = out_copies(5, done + 16, 8, first_pair, second_pair)
 
     def fill(row_cluster, columns, slot, row_from, row_to, col_from, chunk):
-        col_x = columns[0:1, col_from:]
-        col_y = columns[1:2, col_from:]
-        col_z = columns[2:3, col_from:]
+        col_x = pos_c[columns, 0:1, col_from:]
+        col_y = pos_c[columns, 1:2, col_from:]
+        col_z = pos_c[columns, 2:3, col_from:]
         for begin in range(row_from, row_to, chunk):
             rows = pos_t[row_cluster, begin : begin + chunk, :]
             dx = rows[:, 0:1] - col_x
@@ -227,9 +223,8 @@
     whole = slice(0, CLUSTER)
 
     def self_compute(t, slot):
-        columns = pos_c[t]
         for begin in range(0, CLUSTER, STRIP):
-            fill(t, columns, slot, begin, begin + STRIP, begin, SELF_CHUNK)
+            fill(t, t, slot, begin, begin + STRIP, begin, SELF_CHUNK)
 
     def self_apply(t, slot):
         parts = cw[t]
@@ -255,7 +250,7 @@
 
     def pair_compute(t, slot):
         first, second = pair_of(t)
-        fill(first, pos_c[second], slot, 0, CLUSTER, 0, PAIR_CHUNK)
+        fill(first, second, slot, 0, CLUSTER, 0, PAIR_CHUNK)
 
     def pair_apply(t, slot):
         first, second = pair_of(t)
@@ -279,7 +274,6 @@
     def send_first():
         pl.semaphore_wait(barrier, len(peers) + 2)
         start(heads)
-        start(phase1)
 
     def take_heads():
         wait(heads)
@@ -288,29 +282,28 @@
             pos_c[CL_DEV + j, 0:3, :] = next_pos[:, cluster_cols(j)]
 
     def send_last():
-        wait(phase2)
-        start(phase3)
+        wait(phase1)
+        start(phase2)
 
     def send_back():
-        start(give_back)
+        pl.when(gives)(give_back.start)
         start(outs_early)
 
-    section(CL_DEV, self_compute, self_apply, [(2, send_first)])
+    section(CL_DEV, self_compute, self_apply, [(6, send_first), (8, lambda: start(phase1))])
     start(outs_self)
-    wait(phase1)
-    start(phase2)
     section(
         PAIRS,
         pair_compute,
         pair_apply,
-        [(EARLY // 2 - 1, take_heads), (10, send_last), (done // 2, send_back), (done // 2 + 8, lambda: start(outs_late))],
+        [(EARLY // 2 - 1, take_heads), (8, send_last), (done // 2, send_back), (done // 2 + 8, lambda: start(outs_late))],
     )
     start(outs_last)
     wait(outs_self)
     wait(outs_early)
     wait(outs_late)
-    wait(phase3)
-    wait(give_back)
+    wait(phase2)
+    pl.when(gives)(give_back.wait_send)
+    pl.when(gets)(give_back.wait_recv)
     wait(outs_last)
 
 
@@ -385,7 +378,7 @@
         near[local_pairs[1, t]] += second_sum[slot]
         return carry
 
-    lax.fori_loop(0, LOC_DEV, add_local, 0)
+    lax.fori_loop(0, LOC_DEV, add_local, 0, unroll=8)
 
     def add_cross(t, carry):
         near[cross_pairs[0, t]] += first_sum[EARLY + t]
@@ -421,7 +414,7 @@
             jax.ShapeDtypeStruct((CL_DEV, RHS, CLUSTER), F32),
             jax.ShapeDtypeStruct((PAIRS, RHS, CLUSTER), F32),
             jax.ShapeDtypeStruct((PAIRS, RHS, CLUSTER), F32),
-            jax.ShapeDtypeStruct((N_ZC, N_X, N_Y, ROWS, 128), F32),
+            jax.ShapeDtypeStruct((N_ZC, N_Y * N_X, ROWS, 128), F32),
             jax.ShapeDtypeStruct((CROSS_DEV, RHS, CLUSTER), F32),
             jax.ShapeDtypeStruct((8, 128), jnp.int32),
             jax.ShapeDtypeStruct((CL_DEV, 128), F32),
@@ -443,15 +436,14 @@
             floats(FAR_DEV, 128),
             floats(FAR_DEV, 128),
             floats(DEVICES * ROWS, 128),
-            floats(N_Y, N_X * N_ZC * ROWS, 128),
-            floats(N_X, N_Y, N_ZC * ROWS, 128),
+            floats(N_Y * N_X, N_ZC * ROWS, 128),
             floats(RHS, EDGE_PANELS),
             floats(3, EDGE_PANELS),
             floats(RHS, EDGE_PANELS),
             pltpu.VMEM((8, 128), jnp.int32),
         ]
         + [pltpu.VMEM((CLUSTER, CLUSTER), BF16)] * 4
-        + [pltpu.SemaphoreType.DMA((count,)) for count in (4, 13, 13, 3, 4, 4, 7)],
+        + [pltpu.SemaphoreType.DMA((count,)) for count in (4, 22, 22, 2, 4, 4, 7)],
         compiler_params=pltpu.CompilerParams(
             collective_id=0, has_side_effects=True, vmem_limit_bytes=60 * 2**20
         ),

time: 54.3 us -> 52 us (0.958)
  Pallas kernels: 53.4 us -> 51 us
    pallas_call x1, Pallas kernels: 48.6 us -> 46.1 us  [on_device(): pl.pallas_call(near_kernel, out_shape=[jax.ShapeDtypeStruct((CL_DEV, RHS,...]
where the time goes in v5:
time: 52 us; the launch traced here: 51.6 us
  Pallas kernels  51 us (98%)
  between operations  0.66 us (1%)
    pallas_call x1, Pallas kernels, on_device(): pl.pallas_call(near_kernel, out_shape=[jax.ShapeDtypeStruct((CL_DEV, RHS,...  46.1 us
    pallas_call x1, Pallas kernels, on_device(): pl.pallas_call(far_kernel, out_shape=jax.ShapeDtypeStruct((RHS, panels),...  4.86 us

profile of v5, /device:TPU:0, one launch (start us, length us, event | category | flops | bytes accessed | tf_op | source)
XLA Modules:
  0.0 51.6 jit_solution(16622468702334377280)
XLA Ops:
  0.7 46.1 %shard_map.91 = (f32[32,8,512]{2,1,0:T(8,128)}, f32[48,8,512]{2,1,0:T(8,128)}, f32[48,8,512]{2,1,0:T(8,128)}, f32[8,16,8,128]{3,2,1,0:T(8,128)}, f32[16,8,512]{2...) custom-call(f32[3,16384]{1,0:T(4,128)} %pos_hbm.1, f32[1,16384]{1,0:T(1,128)} %bitcast.3, f32[8,16384]{1,0:T(8,128)} %charges_hbm.1, ...), custom_call_target="tpu_custom_call" | custom-call | tf_op jit(solution)/shard_map/pallas_call | solution.py:411
  46.8 4.9 %shard_map.92 = f32[8,16384]{1,0:T(8,128)} custom-call(f32[1024,128]{1,0:T(8,128)} %bitcast.2, f32[32,128]{1,0:T(8,128)} %get-tuple-element.13.proxy_table, f32[16,16384]{1,0:T(8,128)} %basis_hbm.3, f32[1,16384]{1,0:T(1,128)} %bitcast.4, f32[32,8,512]{2,1,0:T(8,128)} %get-tuple-element.14.self_hbm, f32[48,8,512]{2,1,0:T(8,128)} %get-tuple-element.15.first_hbm, ...), custom_call_target="tpu_custom_call" | custom-call | tf_op jit(solution)/shard_map/pallas_call | solution.py:454

commit v6 on v5

--- a/solution.py
+++ b/solution.py
@@ -257,19 +257,22 @@
         first_sum[t] = halves(cw[second], slot, whole, whole, 1)
         second_sum[t] = halves(cw[first], slot, whole, whole, 0)
 
-    def section(count, compute, apply, steps):
-        compute(0, 0)
+    def section(count, compute, apply, steps, after):
 
         def body(i, carry):
             for at, step in steps:
                 pl.when(i == at)(step)
             compute(2 * i + 1, 1)
             apply(2 * i, 0)
-            compute(jnp.minimum(2 * i + 2, count - 1), 0)
+            compute(2 * i + 2, 0)
             apply(2 * i + 1, 1)
             return carry
 
-        lax.fori_loop(0, count // 2, body, 0)
+        lax.fori_loop(0, count // 2 - 1, body, 0)
+        compute(count - 1, 1)
+        apply(count - 2, 0)
+        after()
+        apply(count - 1, 1)
 
     def send_first():
         pl.semaphore_wait(barrier, len(peers) + 2)
@@ -289,13 +292,15 @@
         pl.when(gives)(give_back.start)
         start(outs_early)
 
-    section(CL_DEV, self_compute, self_apply, [(6, send_first), (8, lambda: start(phase1))])
+    self_compute(0, 0)
+    section(CL_DEV, self_compute, self_apply, [(6, send_first), (8, lambda: start(phase1))], lambda: pair_compute(0, 0))
     start(outs_self)
     section(
         PAIRS,
         pair_compute,
         pair_apply,
         [(EARLY // 2 - 1, take_heads), (8, send_last), (done // 2, send_back), (done // 2 + 8, lambda: start(outs_late))],
+        lambda: None,
     )
     start(outs_last)
     wait(outs_self)
@@ -308,27 +313,33 @@
 
 
 def far_kernel(
-    far_hbm, proxy_table, basis_hbm, weight_hbm, self_hbm, first_hbm, second_hbm, returned_hbm,
-    local_pairs, cross_pairs, cross_count, info_in,
-    out, near, far_in, basis, weight, self_sum, first_sum, second_sum, returned, coef, target, coupling, contrib, load_sem,
+    far_hbm, table_hbm, basis_hbm, weight_hbm, self_hbm, first_hbm, second_hbm, returned_hbm,
+    local_hbm, cross_hbm, count_hbm, info_hbm,
+    out, proxy_table, local_pairs, cross_pairs, cross_count, info_in, near, far_in, basis, weight, self_sum, first_sum, second_sum, returned, coef, target, coupling, contrib, load_sem,
 ):
     loads = [
         pltpu.make_async_copy(source, target, load_sem.at[i])
         for i, (source, target) in enumerate(
             (
                 (far_hbm, far_in),
+                (table_hbm, proxy_table),
                 (basis_hbm, basis),
                 (self_hbm, self_sum),
                 (first_hbm, first_sum),
                 (second_hbm, second_sum),
                 (returned_hbm, returned),
                 (weight_hbm, weight),
+                (local_hbm, local_pairs),
+                (cross_hbm, cross_pairs),
+                (count_hbm, cross_count),
+                (info_hbm, info_in),
             )
         )
     ]
     for load in loads:
         load.start()
-    loads[0].wait()
+    for load in loads[:2]:
+        load.wait()
 
     def strided(j):
         return far_in[pl.ds(j, DEVICES, stride=ROWS), :]
@@ -364,7 +375,7 @@
     rows = sum(dot(part, narrow, (1, 0)) for part in split(wide, 3))
     rows_high = rows.astype(BF16).astype(F32)
     lefts = jnp.concatenate([rows_high, rows_high, rows - rows_high], axis=1)
-    for load in loads[1:]:
+    for load in loads[2:]:
         load.wait()
     for c in range(CL_DEV):
         block = basis[:, cluster_cols(c)]
@@ -407,6 +418,9 @@
 
     def floats(*shape):
         return pltpu.VMEM(shape, F32)
+
+    def numbers(*shape):
+        return pltpu.SMEM(shape, jnp.int32)
 
     outs = pl.pallas_call(
         near_kernel,
@@ -454,9 +468,14 @@
     return pl.pallas_call(
         far_kernel,
         out_shape=jax.ShapeDtypeStruct((RHS, panels), F32),
-        in_specs=[hbm, vmem] + [hbm] * 6 + [smem] * 4,
+        in_specs=[hbm] * 12,
         out_specs=vmem,
         scratch_shapes=[
+            floats(CL_DEV, 128),
+            numbers(2, LOC_DEV),
+            numbers(2, CROSS_DEV),
+            numbers(1),
+            numbers(8, 128),
             floats(CL_DEV, RHS, CLUSTER),
             floats(DEVICES * ROWS, 128),
             floats(RANK, panels),
@@ -469,7 +488,7 @@
             floats(128, FAR_DEV),
             floats(RANK * RANK, FAR_DEV),
             floats(128, FAR_DEV),
-            pltpu.SemaphoreType.DMA((7,)),
+            pltpu.SemaphoreType.DMA((12,)),
         ],
         compiler_params=pltpu.CompilerParams(vmem_limit_bytes=60 * 2**20),
     )(

time: 52 us -> 50.8 us (0.977)
  Pallas kernels: 51 us -> 49.7 us
    pallas_call x1, Pallas kernels: 4.86 us -> 3.98 us  [on_device(): pl.pallas_call(far_kernel, out_shape=jax.ShapeDtypeStruct((RHS, panels),...]
where the time goes in v6:
time: 50.8 us; the launch traced here: 50.4 us
  Pallas kernels  49.7 us (98%)
  between operations  0.66 us (1%)
    pallas_call x1, Pallas kernels, on_device(): pl.pallas_call(near_kernel, out_shape=[jax.ShapeDtypeStruct((CL_DEV, RHS,...  45.7 us
    pallas_call x1, Pallas kernels, on_device(): pl.pallas_call(far_kernel, out_shape=jax.ShapeDtypeStruct((RHS, panels),...  3.98 us

profile of v6, /device:TPU:0, one launch (start us, length us, event | category | flops | bytes accessed | tf_op | source)
XLA Modules:
  0.0 50.4 jit_solution(2102265843192404681)
XLA Ops:
  0.7 45.7 %shard_map.91 = (f32[32,8,512]{2,1,0:T(8,128)}, f32[48,8,512]{2,1,0:T(8,128)}, f32[48,8,512]{2,1,0:T(8,128)}, f32[8,16,8,128]{3,2,1,0:T(8,128)}, f32[16,8,512]{2...) custom-call(f32[3,16384]{1,0:T(4,128)} %pos_hbm.1, f32[1,16384]{1,0:T(1,128)} %bitcast.3, f32[8,16384]{1,0:T(8,128)} %charges_hbm.1, ...), custom_call_target="tpu_custom_call" | custom-call | tf_op jit(solution)/shard_map/pallas_call | solution.py:425
  46.4 4.0 %shard_map.92 = f32[8,16384]{1,0:T(8,128)} custom-call(f32[1024,128]{1,0:T(8,128)} %bitcast.2, f32[32,128]{1,0:T(8,128)} %get-tuple-element.13.table_hbm, f32[16,16384]{1,0:T(8,128)} %basis_hbm.3, f32[1,16384]{1,0:T(1,128)} %bitcast.4, f32[32,8,512]{2,1,0:T(8,128)} %get-tuple-element.14.self_hbm, f32[48,8,512]{2,1,0:T(8,128)} %get-tuple-element.15.first_hbm, ...), custom_call_target="tpu_custom_call" | custom-call | tf_op jit(solution)/shard_map/pallas_call | solution.py:468

commit v7 on v6

--- a/solution.py
+++ b/solution.py
@@ -64,8 +64,8 @@
 
 def near_kernel(
     pos_hbm, weight_hbm, charges_hbm, basis_hbm, proxies, far_blocks, cross_vector, local_pairs, cross_pairs, cross_count,
-    self_out, first_out, second_out, far_in, returned, info_in, proxy_table,
-    self_sum, first_sum, second_sum, pos, weight, charges, basis, cw, pos_c, pos_t, moments, coef_rows, proxy_rows, send, recv, head_w, next_pos, next_w,
+    self_out, first_out, second_out, far_in, returned, info_in, table_out,
+    proxy_table, self_sum, first_sum, second_sum, pos, weight, charges, basis, cw, pos_c, pos_t, moments, coef_rows, proxy_rows, send, recv, head_w, next_pos, next_w,
     info, hi0, hi1, lo0, lo1, load_sem, far_send, far_recv, far_own, edge_send, edge_recv, out_sem,
 ):
     y = lax.axis_index("gx")
@@ -111,6 +111,8 @@
     gather = ones_where(row == lane // RANK)
     table = sum(dot(gather, part, (1, 0)) for part in split(spread, 3))
     proxy_table[...] = table
+    out_table = pltpu.make_async_copy(proxy_table, table_out, out_sem.at[7])
+    out_table.start()
 
     for load in loads:
         load.wait()
@@ -303,6 +305,7 @@
         lambda: None,
     )
     start(outs_last)
+    out_table.wait()
     wait(outs_self)
     wait(outs_early)
     wait(outs_late)
@@ -434,8 +437,9 @@
             jax.ShapeDtypeStruct((CL_DEV, 128), F32),
         ],
         in_specs=[hbm] * 4 + [vmem] * 3 + [smem] * 3,
-        out_specs=[hbm] * 6 + [vmem],
+        out_specs=[hbm] * 7,
         scratch_shapes=[
+            floats(CL_DEV, 128),
             floats(CL_DEV, RHS, CLUSTER),
             floats(PAIRS, RHS, CLUSTER),
             floats(PAIRS, RHS, CLUSTER),
@@ -457,7 +461,7 @@
             pltpu.VMEM((8, 128), jnp.int32),
         ]
         + [pltpu.VMEM((CLUSTER, CLUSTER), BF16)] * 4
-        + [pltpu.SemaphoreType.DMA((count,)) for count in (4, 22, 22, 2, 4, 4, 7)],
+        + [pltpu.SemaphoreType.DMA((count,)) for count in (4, 22, 22, 2, 4, 4, 8)],
         compiler_params=pltpu.CompilerParams(
             collective_id=0, has_side_effects=True, vmem_limit_bytes=60 * 2**20
         ),

time: 50.8 us -> 50.2 us (0.988)
  Pallas kernels: 49.7 us -> 49.1 us
    pallas_call x1, Pallas kernels: 45.7 us -> 45.1 us  [on_device(): pl.pallas_call(near_kernel, out_shape=[jax.ShapeDtypeStruct((CL_DEV, RHS,...]
where the time goes in v7:
time: 50.2 us; the launch traced here: 49.7 us
  Pallas kernels  49.1 us (98%)
  between operations  0.66 us (1%)
    pallas_call x1, Pallas kernels, on_device(): pl.pallas_call(near_kernel, out_shape=[jax.ShapeDtypeStruct((CL_DEV, RHS,...  45.1 us
    pallas_call x1, Pallas kernels, on_device(): pl.pallas_call(far_kernel, out_shape=jax.ShapeDtypeStruct((RHS, panels),...  3.97 us

profile of v7, /device:TPU:0, one launch (start us, length us, event | category | flops | bytes accessed | tf_op | source)
XLA Modules:
  0.0 49.7 jit_solution(17700287807425155073)
XLA Ops:
  0.7 45.1 %shard_map.91 = (f32[32,8,512]{2,1,0:T(8,128)}, f32[48,8,512]{2,1,0:T(8,128)}, f32[48,8,512]{2,1,0:T(8,128)}, f32[8,16,8,128]{3,2,1,0:T(8,128)}, f32[16,8,512]{2...) custom-call(f32[3,16384]{1,0:T(4,128)} %pos_hbm.1, f32[1,16384]{1,0:T(1,128)} %bitcast.3, f32[8,16384]{1,0:T(8,128)} %charges_hbm.1, ...), custom_call_target="tpu_custom_call" | custom-call | tf_op jit(solution)/shard_map/pallas_call | solution.py:428
  45.8 4.0 %shard_map.92 = f32[8,16384]{1,0:T(8,128)} custom-call(f32[1024,128]{1,0:T(8,128)} %bitcast.2, f32[32,128]{1,0:T(8,128)} %get-tuple-element.13.table_hbm, f32[16,16384]{1,0:T(8,128)} %basis_hbm.3, f32[1,16384]{1,0:T(1,128)} %bitcast.4, f32[32,8,512]{2,1,0:T(8,128)} %get-tuple-element.14.self_hbm, f32[48,8,512]{2,1,0:T(8,128)} %get-tuple-element.15.first_hbm, ...), custom_call_target="tpu_custom_call" | custom-call | tf_op jit(solution)/shard_map/pallas_call | solution.py:472

commit v8 on v7

--- a/solution.py
+++ b/solution.py
@@ -78,7 +78,7 @@
     loads = [
         pltpu.make_async_copy(source, target, load_sem.at[i])
         for i, (source, target) in enumerate(
-            ((weight_hbm, weight), (charges_hbm, charges), (pos_hbm, pos), (basis_hbm, basis))
+            ((pos_hbm, pos), (weight_hbm, weight), (charges_hbm, charges), (basis_hbm, basis))
         )
     ]
     for load in loads:
@@ -114,7 +114,7 @@
     out_table = pltpu.make_async_copy(proxy_table, table_out, out_sem.at[7])
     out_table.start()
 
-    for load in loads:
+    for load in loads[:3]:
         load.wait()
     for c in range(CL_DEV):
         cols = cluster_cols(c)
@@ -123,8 +123,10 @@
         place = jnp.concatenate([pos[:, cols], jnp.zeros((5, CLUSTER), F32)], axis=0)
         pos_c[c] = place
         pos_t[c] = place.T
-        moments[c * 32 : (c + 1) * 32, :] = dot(split_rows(basis[:, cols]), parts, (1, 1))
     head_w[...] = charges[:, :EDGE_PANELS] * weight[:, :EDGE_PANELS]
+    loads[3].wait()
+    for c in range(CL_DEV):
+        moments[c * 32 : (c + 1) * 32, :] = dot(split_rows(basis[:, cluster_cols(c)]), cw[c], (1, 1))
 
     row, lane = iotas((2 * RHS, 128))
     spread = ones_where(lax.rem(row, RHS) == lax.rem(lane, RHS))

time: 50.2 us -> 50.6 us (level)
  no operation moved by 1% of the time
where the time goes in v8:
time: 50.6 us; the launch traced here: 50.2 us
  Pallas kernels  49.6 us (98%)
  between operations  0.66 us (1%)
    pallas_call x1, Pallas kernels, on_device(): pl.pallas_call(near_kernel, out_shape=[jax.ShapeDtypeStruct((CL_DEV, RHS,...  45.6 us
    pallas_call x1, Pallas kernels, on_device(): pl.pallas_call(far_kernel, out_shape=jax.ShapeDtypeStruct((RHS, panels),...  3.98 us

profile of v8, /device:TPU:0, one launch (start us, length us, event | category | flops | bytes accessed | tf_op | source)
XLA Modules:
  0.0 50.2 jit_solution(1339719132974253454)
XLA Ops:
  0.7 45.6 %shard_map.91 = (f32[32,8,512]{2,1,0:T(8,128)}, f32[48,8,512]{2,1,0:T(8,128)}, f32[48,8,512]{2,1,0:T(8,128)}, f32[8,16,8,128]{3,2,1,0:T(8,128)}, f32[16,8,512]{2...) custom-call(f32[3,16384]{1,0:T(4,128)} %pos_hbm.1, f32[1,16384]{1,0:T(1,128)} %bitcast.3, f32[8,16384]{1,0:T(8,128)} %charges_hbm.1, ...), custom_call_target="tpu_custom_call" | custom-call | tf_op jit(solution)/shard_map/pallas_call | solution.py:430
  46.2 4.0 %shard_map.92 = f32[8,16384]{1,0:T(8,128)} custom-call(f32[1024,128]{1,0:T(8,128)} %bitcast.2, f32[32,128]{1,0:T(8,128)} %get-tuple-element.13.table_hbm, f32[16,16384]{1,0:T(8,128)} %basis_hbm.3, f32[1,16384]{1,0:T(1,128)} %bitcast.4, f32[32,8,512]{2,1,0:T(8,128)} %get-tuple-element.14.self_hbm, f32[48,8,512]{2,1,0:T(8,128)} %get-tuple-element.15.first_hbm, ...), custom_call_target="tpu_custom_call" | custom-call | tf_op jit(solution)/shard_map/pallas_call | solution.py:474
